TPU v7x, 256 devices: a whole 4x4x8 slice. The times are simulated.
256 devices in a mesh: dp: 8 (over y, z_hi), ctx: 32 (over z_lo, x, core).
Axes of the slice: x: 4, y: 4, z: 8 (z_hi: 2, z_lo: 4; z = z_hi * 4 + z_lo), core: 2. Of those that a mesh axis runs over, the one named last changes fastest.
Arguments:
- hidden_state: bfloat16 [8, 32768, 1536], P('dp', 'ctx'), may hold values from -45 to 45
- tokens: int32 [8, 32768], P('dp', 'ctx'), may hold values from 0 to 4
- in_codes: bfloat16 [24, 32, 1536], P('dp'), may hold values from -0.21875 to 0.21875
- in_scales: float32 [24, 12], P('dp'), may hold values from 0.5 to 2
- out_codes: bfloat16 [24, 32, 768], P('dp'), may hold values from -0.21875 to 0.21875
- out_scales: float32 [24, 6], P('dp'), may hold values from 0.5 to 2
- short_filter: bfloat16 [4, 768], replicated, may hold values from -3 to 3
- long_filter: bfloat16 [128, 768], replicated, may hold values from -0.5 to 0.5
Outputs:
- new_state: bfloat16 [8, 32768, 1536], P('dp', 'ctx')
Inputs may be any that keep to these rules, and one draw needn't show every extreme that they name: `tokens`: values 0 to 3 are the bases A, C, G, T; 4 is an unknown base N.
All inputs are finite; a program needn't handle non-finite values.
Results may differ from a plain program's by a relative error of at most 0.022.
Values may be sent and summed in bfloat16 or wider, within the bound.
A program may use at most 128 MiB of HBM per device.

v0:
```python
import jax
import jax.numpy as jnp
from jax import lax
from jax.sharding import PartitionSpec as P


def passed_along(value, axis, steps):
    count = lax.axis_size(axis)
    first, last = (max(0, -steps), min(count, count - steps))
    return lax.ppermute(value, axis, [(source, source + steps) for source in range(first, last)])


def flip_groups(values, groups):
    shaped = values.reshape((groups, values.shape[0] // groups) + values.shape[1:])
    return shaped[::-1].reshape(values.shape)


def mirror_inward(backward_half, letters):
    groups = lax.axis_size("ctx")
    first_vals, first_letters = (
        lax.all_to_all(backward_half, "ctx", split_axis=0, concat_axis=0, tiled=True),
        lax.all_to_all(letters, "ctx", split_axis=0, concat_axis=0, tiled=True),
    )
    second_vals, second_letters = (
        lax.all_to_all(first_vals[::-1], "ctx", split_axis=0, concat_axis=0, tiled=True),
        lax.all_to_all(first_letters[::-1], "ctx", split_axis=0, concat_axis=0, tiled=True),
    )
    return (flip_groups(second_vals, groups), flip_groups(second_letters, groups))


def mirror_outward(strand_out):
    groups = lax.axis_size("ctx")
    first_vals = lax.all_to_all(strand_out, "ctx", split_axis=0, concat_axis=0, tiled=True)
    second_vals = lax.all_to_all(first_vals[::-1], "ctx", split_axis=0, concat_axis=0, tiled=True)
    return flip_groups(second_vals, groups)


def block_fold(left_part, pieces):
    code_block, scales = pieces
    block_count, block_rows, columns = code_block.shape
    widened = jnp.repeat(scales, columns // scales.shape[1], axis=1)[:, None, :]
    weight = (code_block.astype(jnp.float32) * widened).astype(jnp.bfloat16)
    weight = weight.reshape(block_count * block_rows, columns)
    return jnp.dot(left_part, weight, preferred_element_type=jnp.float32)


def depthwise(values, filter_taps):
    return lax.conv_general_dilated(
        values,
        filter_taps[:, None, :],
        (1,),
        "VALID",
        dimension_numbers=("NWC", "WIO", "NWC"),
        feature_group_count=filter_taps.shape[1],
        preferred_element_type=jnp.float32,
    )


def shards(
    hidden_state, tokens, in_codes, in_scales, out_codes, out_scales, short_filter, long_filter
):
    window = hidden_state[0]
    letters = tokens[0]
    row_count = window.shape[0]
    half_width = window.shape[1] // 2
    inner_width = short_filter.shape[1]
    rim_rows = short_filter.shape[0] + long_filter.shape[0] - 2
    forward = window[:, :half_width]
    forward_keep = (letters != 4).astype(jnp.float32)
    backward, backward_letters = mirror_inward(window[:, half_width:], letters)
    backward_keep = (backward_letters != 4).astype(jnp.float32)
    strands = jnp.stack([forward, backward])
    keep_mask = jnp.stack([forward_keep, backward_keep])
    widened = strands.astype(jnp.float32)
    normed = (
        widened * lax.rsqrt(jnp.mean(widened * widened, axis=-1, keepdims=True) + 1e-05)
    ).astype(jnp.bfloat16)
    normed = normed.reshape(2 * row_count, half_width)
    projected = block_fold(
        normed,
        (
            lax.all_gather(in_codes, "dp", axis=0, tiled=True),
            lax.all_gather(in_scales.astype(jnp.bfloat16), "dp", axis=0, tiled=True).astype(
                jnp.float32
            ),
        ),
    )
    projected = projected.reshape(2, row_count, 2 * inner_width)
    masked = (projected[:, :, :inner_width] * keep_mask[:, :, None]).astype(jnp.bfloat16)
    gate_part = projected[:, :, inner_width:]
    tail_rows = masked[:, row_count - rim_rows :, :]
    rim_values = passed_along(tail_rows, "ctx", 1)
    extended = jnp.concatenate([rim_values, masked], axis=1)
    short_out = depthwise(extended, short_filter).astype(jnp.bfloat16)
    long_out = depthwise(short_out, long_filter)
    blended = (
        (jax.nn.silu(gate_part) * long_out).astype(jnp.bfloat16).reshape(2 * row_count, inner_width)
    )
    branch = block_fold(
        blended,
        (
            lax.all_gather(out_codes, "dp", axis=0, tiled=True),
            lax.all_gather(out_scales.astype(jnp.bfloat16), "dp", axis=0, tiled=True).astype(
                jnp.float32
            ),
        ),
    )
    branch = branch.reshape(2, row_count, half_width)
    forward_out = (forward.astype(jnp.float32) + branch[0]).astype(jnp.bfloat16)
    strand_out = (backward.astype(jnp.float32) + branch[1]).astype(jnp.bfloat16)
    backward_out = mirror_outward(strand_out)
    return jnp.concatenate([forward_out, backward_out], axis=-1)[None]


def solution(mesh):
    in_specs = (
        P("dp", "ctx", None),
        P("dp", "ctx"),
        P("dp", None, None),
        P("dp", None),
        P("dp", None, None),
        P("dp", None),
        P(),
        P(),
    )
    out_specs = P("dp", "ctx", None)
    return jax.shard_map(shards, mesh=mesh, in_specs=in_specs, out_specs=out_specs, check_vma=False)
```

profile of v0, /device:TPU:1, one launch (start us, length us, event | category | flops | bytes accessed | tf_op | source)
XLA Modules:
  0.0 446.8 jit_solution(8172828875166576608)
XLA Ops:
  6.5 0.6 broadcast.78
  7.1 1.4 reduce.6
  8.5 0.7 all_to_all.45
  9.2 10.0 %all-to-all-start.2 = ((s32[32,32,1]{1,2,0:T(1,128)}), s32[32,32,1]{1,2,0:T(1,128)S(1)}, u32[]{:S(2)}, u32[]{:S(2)}) async-start(s32[32,32,1]{1,2,0:T(1,128)} %all_to_all.45), calls=%async_computation.2 | async-start | bytes 32768 | tf_op jit(solution)/shard_map/all_to_all | solution.py:22
  19.2 3.7 slice_bitcast_fusion
  23.0 3.6 all-to-all-done.2
  26.5 4.3 all-to-all-start
  30.8 0.7 all-gather.5.cloned.1.call-update
  31.5 0.7 reduce.7
  32.4 0.7 all_to_all.48
  33.1 41.0 %all-to-all-done = bf16[32,32,768]{2,1,0:T(8,128)(2,1)S(1)} async-done(((bf16[32,32,768]{2,1,0:T(8,128)(2,1)}), bf16[32,32,768]{2,1,0:T(8,128)(2,1)S(1)}, u32[]{:S(2)}, u32[]{:S(2)}) %all-to-all-start) | async-done | bytes 1572896 | tf_op jit(solution)/shard_map/all_to_all | solution.py:21
  74.1 6.2 %all-to-all-start.3 = ((s32[32,32,1]{1,2,0:T(1,128)}), s32[32,32,1]{1,2,0:T(1,128)S(1)}, u32[]{:S(2)}, u32[]{:S(2)}) async-start(s32[32,32,1]{1,2,0:T(1,128)} %all_to_all.48), calls=%async_computation.3 | async-start | bytes 32768 | tf_op jit(solution)/shard_map/all_to_all | solution.py:26
  80.3 15.3 %rev.16 = bf16[1024,768]{1,0:T(8,128)(2,1)} reverse(bf16[1024,768]{1,0:T(8,128)(2,1)S(1)} %bitcast.55), dimensions={0} | reverse | bytes 3145728 | tf_op jit(solution)/shard_map/rev | solution.py:25
  95.6 10.2 %all-to-all-done.3 = s32[32,32,1]{1,2,0:T(1,128)S(1)} async-done(((s32[32,32,1]{1,2,0:T(1,128)}), s32[32,32,1]{1,2,0:T(1,128)S(1)}, u32[]{:S(2)}, u32[]{:S(2)}) %all-to-all-start.3) | async-done | bytes 4128 | tf_op jit(solution)/shard_map/all_to_all | solution.py:26
  105.8 3.9 all-to-all-start.1
  109.7 0.7 all-gather.7.cloned.1.call-update
  110.4 48.3 %all-gather = bf16[8,3,12]{2,1,0:T(4,128)(2,1)S(1)} all-gather(bf16[1,3,12]{2,1,0:T(4,128)(2,1)S(1)} %convert_bitcast_fusion.1), channel_id=1, replica_groups=mesh['dp'=8,'ctx'=32] {'dp'}, dimensions={0}, use_global_device_ids=true | all-gather | bytes 648 | tf_op jit(solution)/shard_map/all_gather | solution.py:83
  158.7 0.1 broadcast_in_dim.17
  158.9 26.6 %all-gather.1 = bf16[8,3,6]{2,1,0:T(4,128)(2,1)S(1)} all-gather(bf16[1,3,6]{2,1,0:T(4,128)(2,1)S(1)} %convert_bitcast_fusion), channel_id=1, replica_groups=mesh['dp'=8,'ctx'=32] {'dp'}, dimensions={0}, use_global_device_ids=true | all-gather | bytes 324 | tf_op jit(solution)/shard_map/all_gather | solution.py:103
  185.7 3.6 multiply_convert_fusion
  189.4 2.6 fusion.11
  192.0 7.3 %fusion.23 = f32[2,1024,1536]{2,1,0:T(8,128)S(1)} fusion(bf16[768,1536,1]{1,0,2:T(8,128)(2,1)} %bitcast.62, f32[2,1024]{1,0:T(2,128)S(1)} %add_rsqrt_fusion, bf16[1,1024,768]{2,1,0:T(8,128)(2,1)S(1)} %bitcast.57, bf16[1,1024,768]{2,1,0:T(8,128)(2,1)} %get-tuple-element.7), kind=kOutput, calls=%fused_computation.31 | convolution fusion | flops 4838129664 | bytes 18096128 | tf_op jit(solution)/shard_map/dot_general | solution.py:44
  199.3 4.5 %copy-done.4 = f32[2,1024,1536]{2,1,0:T(8,128)} copy-done((f32[2,1024,1536]{2,1,0:T(8,128)}, f32[2,1024,1536]{2,1,0:T(8,128)S(1)}, u32[]{:S(2)}) %copy-start.4) | copy-done | bytes 12582936
  203.8 0.4 fusion.14
  204.2 0.9 slice.37
  205.1 9.5 %collective-permute-start = (bf16[2,130,768]{2,1,0:T(8,128)(2,1)}, bf16[2,130,768]{2,1,0:T(8,128)(2,1)}, u32[]{:S(2)}, u32[]{:S(2)}) collective-permute-start(bf16[2,130,768]{2,1,0:T(8,128)(2,1)} %slice.37), channel_id=1, source_target_pairs={{0,1},{1,2},{2,3},{3,4},{4,5},{5,6},{6,7},{7,8},{8,9},{9,10},{10,1... | collective-permute-start | bytes 1198088 | tf_op jit(solution)/shard_map/ppermute | solution.py:10
  214.8 2.5 multiply_convert_fusion.1
  217.4 2.4 collective-permute-done
  219.7 3.1 fusion.21
  222.9 3.8 reshape.111
  226.7 0.9 slice.38
  227.7 2.3 fusion.15
  230.0 4.0 fusion.20
  234.1 0.7 slice.39
  234.8 0.9 fusion.42
  235.7 71.4 %fusion.6 = f32[16,145,768]{2,0,1:T(8,128)S(1)} fusion(bf16[128,1,768]{2,0,1:T(8,128)(2,1)S(1)} %bitcast.51, bf16[16,272,768]{2,0,1:T(8,128)(2,1)S(1)} %fusion.42), kind=kOutput, calls=%fused_computation.12 | convolution fusion | flops 456130560 | bytes 14008320 | tf_op jit(solution)/shard_map/conv_general_dilated | solution.py:48
  307.1 7.1 %copy.28 = f32[16,145,768]{2,1,0:T(8,128)} copy(f32[16,145,768]{2,0,1:T(8,128)S(1)} %fusion.6) | data formatting | bytes 14254080 | tf_op jit(solution)/shard_map/conv_general_dilated | solution.py:48
  314.2 5.6 %reshape.118 = f32[2,1160,768]{2,1,0:T(8,128)} reshape(f32[16,145,768]{2,1,0:T(8,128)} %copy.28) | data formatting | bytes 14254080 | tf_op jit(solution)/shard_map/conv_general_dilated | solution.py:48
  319.8 5.6 %fusion.13 = bf16[2,1024,768]{2,1,0:T(8,128)(2,1)S(1)} fusion(f32[2,1160,768]{2,1,0:T(8,128)} %reshape.118, f32[2,1024,1536]{2,1,0:T(8,128)} %copy-done.4), kind=kLoop, calls=%fused_computation.19 | loop fusion | flops 9437184 | bytes 15728640 | tf_op jit(solution)/shard_map/convert_element_type | solution.py:97
  325.4 2.8 fusion.35
  328.2 0.6 fusion.25
  328.8 0.8 copy-done.3
  329.6 0.5 add_convert_fusion
  330.1 47.0 %all_to_all.60 = bf16[32,32,768]{2,1,0:T(8,128)(2,1)S(1)} all-to-all(bf16[32,32,768]{2,1,0:T(8,128)(2,1)S(1)} %add_convert_fusion), channel_id=1, replica_groups=mesh['dp'=8,'ctx'=32] {'ctx'}, dimensions={0} | all-to-all | bytes 3145728 | tf_op jit(solution)/shard_map/all_to_all | solution.py:33
  377.1 15.2 %rev.20 = bf16[1024,768]{1,0:T(8,128)(2,1)} reverse(bf16[1024,768]{1,0:T(8,128)(2,1)S(1)} %bitcast.58), dimensions={0} | reverse | bytes 3145728 | tf_op jit(solution)/shard_map/rev | solution.py:34
  392.3 43.0 %all_to_all.61 = bf16[32,32,768]{2,1,0:T(8,128)(2,1)S(1)} all-to-all(bf16[32,32,768]{2,1,0:T(8,128)(2,1)} %bitcast.59), channel_id=1, replica_groups=mesh['dp'=8,'ctx'=32] {'ctx'}, dimensions={0} | all-to-all | bytes 3145728 | tf_op jit(solution)/shard_map/all_to_all | solution.py:34
  435.4 1.3 reverse.4
  436.7 3.3 maximum_bitcast_fusion
  (45 shorter events, 0.8 us)
Async XLA Ops:
  6.5 229.1 %copy-start = (bf16[128,768]{1,0:T(8,128)(2,1)S(1)}, bf16[128,768]{1,0:T(8,128)(2,1)}, u32[]{:S(2)}) copy-start(bf16[128,768]{1,0:T(8,128)(2,1)} %param.15) | copy-start | bytes 589828
  9.2 17.3 %all-to-all-start.2 = ((s32[32,32,1]{1,2,0:T(1,128)}), s32[32,32,1]{1,2,0:T(1,128)S(1)}, u32[]{:S(2)}, u32[]{:S(2)}) async-start(s32[32,32,1]{1,2,0:T(1,128)} %all_to_all.45), calls=%async_computation.2 | async-start | bytes 32768 | tf_op jit(solution)/shard_map/all_to_all | solution.py:22
  26.5 47.6 %all-to-all-start = ((bf16[32,32,768]{2,1,0:T(8,128)(2,1)}), bf16[32,32,768]{2,1,0:T(8,128)(2,1)S(1)}, u32[]{:S(2)}, u32[]{:S(2)}) async-start(bf16[32,32,768]{2,1,0:T(8,128)(2,1)} %bitcast.2), calls=%async_computation | async-start | bytes 3145728 | tf_op jit(solution)/shard_map/all_to_all | solution.py:21
  30.8 79.6 %copy-start.8 = (f32[3,12]{1,0:T(4,128)S(1)}, f32[3,12]{1,0:T(4,128)}, u32[]{:S(2)}) copy-start(f32[3,12]{1,0:T(4,128)} %param.11) | copy-start | bytes 436
  30.8 154.9 %all-gather.5.cloned.1.call-start = ((), (), s32[]{:S(2)}) async-start(), calls=%async_computation.6 | async-start | bytes 2654208 | tf_op jit(solution)/shard_map/all_gather | solution.py:82
  32.3 126.7 %copy-start.9 = (f32[3,6]{1,0:T(4,128)S(1)}, f32[3,6]{1,0:T(4,128)}, u32[]{:S(2)}) copy-start(f32[3,6]{1,0:T(4,128)} %param.13) | copy-start | bytes 220
  32.3 153.3 %copy-start.7 = (s32[1,1024]{1,0:T(1,128)S(1)}, s32[1,1024]{1,0:T(1,128)}, u32[]{:S(2)}) copy-start(s32[1,1024]{1,0:T(1,128)} %param.9) | copy-start | bytes 12292
  74.1 31.7 %all-to-all-start.3 = ((s32[32,32,1]{1,2,0:T(1,128)}), s32[32,32,1]{1,2,0:T(1,128)S(1)}, u32[]{:S(2)}, u32[]{:S(2)}) async-start(s32[32,32,1]{1,2,0:T(1,128)} %all_to_all.48), calls=%async_computation.3 | async-start | bytes 32768 | tf_op jit(solution)/shard_map/all_to_all | solution.py:26
  105.8 83.5 %all-to-all-start.1 = ((bf16[32,32,768]{2,1,0:T(8,128)(2,1)}), bf16[32,32,768]{2,1,0:T(8,128)(2,1)S(1)}, u32[]{:S(2)}, u32[]{:S(2)}) async-start(bf16[32,32,768]{2,1,0:T(8,128)(2,1)} %bitcast.4), calls=%async_computation.1 | async-start | bytes 3145728 | tf_op jit(solution)/shard_map/all_to_all | solution.py:25
  109.7 105.2 %all-gather.7.cloned.1.call-start = ((), (), s32[]{:S(2)}) async-start(), calls=%async_computation.7 | async-start | bytes 1327104 | tf_op jit(solution)/shard_map/all_gather | solution.py:102
  189.3 2.7 copy-start.2
  199.3 4.5 %copy-start.4 = (f32[2,1024,1536]{2,1,0:T(8,128)}, f32[2,1024,1536]{2,1,0:T(8,128)S(1)}, u32[]{:S(2)}) copy-start(f32[2,1024,1536]{2,1,0:T(8,128)S(1)} %fusion.23) | copy-start | bytes 37748740
  205.1 14.6 %collective-permute-start = (bf16[2,130,768]{2,1,0:T(8,128)(2,1)}, bf16[2,130,768]{2,1,0:T(8,128)(2,1)}, u32[]{:S(2)}, u32[]{:S(2)}) collective-permute-start(bf16[2,130,768]{2,1,0:T(8,128)(2,1)} %slice.37), channel_id=1, source_target_pairs={{0,1},{1,2},{2,3},{3,4},{4,5},{5,6},{6,7},{7,8},{8,9},{9,10},{10,1... | collective-permute-start | bytes 1198088 | tf_op jit(solution)/shard_map/ppermute | solution.py:10
  227.6 2.4 copy-start.10
  227.7 2.4 copy-start.11
  319.8 5.6 %copy-start.6 = (bf16[24,32,768]{2,1,0:T(8,128)(2,1)S(1)}, bf16[24,32,768]{2,1,0:T(8,128)(2,1)}, u32[]{:S(2)}) copy-start(bf16[24,32,768]{2,1,0:T(8,128)(2,1)} %multiply_convert_fusion.1) | copy-start | bytes 3538948
  325.4 2.8 copy-start.5
  328.2 1.4 copy-start.3
  435.4 4.6 %copy-start.1 = (bf16[128,768]{1,0:T(8,128)(2,1)S(1)}, bf16[128,768]{1,0:T(8,128)(2,1)}, u32[]{:S(2)}) copy-start(bf16[128,768]{1,0:T(8,128)(2,1)} %param.15) | copy-start | bytes 589828
Sparse Core Ops, SparseCore 0:
  34.2 81.8 all-gather.4
  118.7 61.2 all-gather.6
where the time goes:
time: 448 us; the launch traced here: 447 us
  blocking collectives  165 us (37%)
  matrix products  85.5 us (19%)
  local copies, waits for them, and re-layouts  62.6 us (14%)
  waiting for transfers between devices  58.5 us (13%)
  starting transfers between devices  33.9 us (8%)
  other arithmetic  27.6 us (6%)
  between operations  13.8 us (3%)
    conv_general_dilated x2, matrix products, depthwise(): lax.conv_general_dilated(values, filter_taps[:, None, :], (1,), 'VALID',...  75.4 us
    all_gather x1, blocking collectives, shards(): lax.all_gather(in_scales.astype(jnp.bfloat16), 'dp', axis=0, tiled=True)  48.3 us
    all_to_all x1, blocking collectives, mirror_outward(): lax.all_to_all(strand_out, 'ctx', split_axis=0, concat_axis=0, tiled=True)  47 us
    all_to_all x1, blocking collectives, mirror_outward(): lax.all_to_all(first_vals[::-1], 'ctx', split_axis=0, concat_axis=0, tile...  43 us
    all_to_all x1, waiting for transfers between devices, mirror_inward(): lax.all_to_all(backward_half, 'ctx', split_axis=0, concat_axis=0, tiled=T...  41 us
    all_gather x1, blocking collectives, shards(): lax.all_gather(out_scales.astype(jnp.bfloat16), 'dp', axis=0, tiled=True)  26.6 us
    conv_general_dilated x4, local copies, waits for them, and re-layouts, depthwise(): lax.conv_general_dilated(values, filter_taps[:, None, :], (1,), 'VALID',...  17.4 us
    rev x1, local copies, waits for them, and re-layouts, mirror_inward(): first_vals[::-1]  15.3 us
  transfers between devices with their start and end apart: 7, of which 4 were waited for; matrix products, arithmetic and copies ran while one was open for 8% of the time, Pallas kernels for 0%

commit v1 on v0

v1 whole, which is shorter than its diff:
```python
import functools

import jax
import jax.numpy as jnp
import numpy as np
from jax import lax
from jax.experimental import pallas as pl
from jax.experimental.pallas import tpu as pltpu
from jax.sharding import PartitionSpec as P

MESH = pl.DeviceIdType.MESH
F32, BF16 = jnp.float32, jnp.bfloat16
ROWS, HALO = 1024, 144
WIDTH, SHARD = 768, 96
BLOCK, SPAN = 128, 256
TILE = 256
DP, CTX = 8, 32
LONG, SHORT = 128, 4
VMEM_LIMIT = 63 << 20


def transform(positions):
    freq = np.arange(BLOCK)[:, None]
    angle = 2 * np.pi * ((freq * positions[None, :]) % SPAN) / SPAN
    real, imag = np.cos(angle), -np.sin(angle)
    imag[0] = np.cos(np.pi * (positions % 2))
    return np.concatenate([real, imag], axis=0)


def split(matrix):
    high = matrix.astype(np.float32).astype(BF16)
    return high, (matrix - high.astype(np.float64)).astype(np.float32).astype(BF16)


def constants():
    spread = transform(np.arange(SPAN))
    long_high, long_low = split(transform(LONG - 1 - np.arange(LONG)))
    short_table = np.zeros((SPAN, 16))
    short_table[:, :SHORT] = transform(SHORT - 1 - np.arange(SHORT))
    short_high, short_low = split(short_table)
    as_bf16 = lambda table: table.astype(np.float32).astype(BF16)
    gather_forward = as_bf16(spread[:, BLOCK:].T)
    gather_backward = as_bf16(spread[:, :BLOCK].T)
    return (
        as_bf16(spread),
        gather_forward,
        gather_backward,
        long_high,
        long_low,
        short_high,
        short_low,
    )


def layer_kernel(
    hidden,
    tokens,
    in_codes,
    in_scales,
    out_codes,
    out_scales,
    short_source,
    long_source,
    spread_source,
    gather_forward_source,
    gather_backward_source,
    long_high_source,
    long_low_source,
    short_high_source,
    short_low_source,
    out,
    weights,
    codes,
    last_codes,
    scales,
    last_scales,
    letters,
    token_forward,
    token_backward,
    halo_forward,
    halo_backward,
    short_filter,
    long_filter,
    spread,
    gather_forward,
    gather_backward,
    long_high,
    long_low,
    short_high,
    short_low,
    state,
    normed,
    masked_forward,
    masked_backward,
    keep,
    pure,
    cross,
    edge,
    taps,
    conv,
    load_sem,
    store_sem,
    piece_recv,
    cross_recv,
    mate_recv,
    halo_recv,
    z_send,
    y_send,
    x_send,
    mate_send,
    halo_send,
):
    dp, ctx = lax.axis_index("dp"), lax.axis_index("ctx")
    y, z_high = dp // 2, dp % 2
    z_low, x, core = ctx // 8, (ctx // 2) % 4, ctx % 2
    half = x % 2
    partner = dp + 1 - 2 * z_high
    ring = 4
    below, above, across = (y + 3) % ring, (y + 1) % ring, (y + 2) % ring
    up, down = ((dp + 2) % DP, ctx), ((dp + DP - 2) % DP, ctx)
    opposite = ((dp + 4) % DP, ctx)
    step = 1 - 2 * core
    beside = (dp, z_low * 8 + (x + ring + step) % ring * 2 + core)
    beside_source = (dp, z_low * 8 + (x + ring - step) % ring * 2 + core)
    mate = (dp, ctx + step)
    after, before = (dp, (ctx + 1) % CTX), (dp, (ctx + CTX - 1) % CTX)
    border = z_low // 3 + (3 - z_low) // 3
    fetches = (core + z_high) % 2

    loads = []

    def load(source, target):
        index = len(loads)
        copy = pltpu.make_async_copy(source, target, load_sem.at[index])
        copy.start()
        loads.append(copy)
        return copy

    code_loads = [load(in_codes, codes), load(in_scales, scales)]
    last_loads = [load(out_codes, last_codes), load(out_scales, last_scales)]
    letter_load = load(tokens, letters)
    filter_loads = [
        load(short_source, short_filter),
        load(long_source, long_filter),
        load(long_high_source, long_high),
        load(long_low_source, long_low),
        load(short_high_source, short_high),
        load(short_low_source, short_low),
    ]
    state_loads = [
        load(hidden.at[:, pl.ds(strand * WIDTH, WIDTH)], state.at[strand]) for strand in range(2)
    ]
    table_loads = [
        load(spread_source, spread),
        load(gather_forward_source, gather_forward),
        load(gather_backward_source, gather_backward),
    ]

    barrier = pltpu.get_barrier_semaphore()
    for device in (up, down, opposite, beside_source, mate, after, before):
        pl.semaphore_signal(barrier, inc=1, device_id=device, device_id_type=MESH)

    @pl.when(fetches == 1)
    def _():
        shift = (z_low // 2) * 24
        source = (partner, ctx + 24 - 8 * z_low - shift)
        pl.semaphore_signal(barrier, inc=1, device_id=source, device_id_type=MESH)

    def dequantise(part):
        for block in range(3):
            rows = pl.ds(pl.multiple_of(dp * SHARD + block * 32, 32), 32)
            for group in range(6):
                column = group * 128
                if part < 2:
                    place = part * 6 + group
                    values = codes[block, :, place * 128 : place * 128 + 128]
                    scale = scales[block : block + 1, place : place + 1]
                else:
                    values = last_codes[block, :, column : column + 128]
                    scale = last_scales[block : block + 1, group : group + 1]
                weights[part, rows, column : column + 128] = (values.astype(F32) * scale).astype(BF16)

    for copy in code_loads:
        copy.wait()
    dequantise(0)
    pl.semaphore_wait(barrier, 7 + 2 * border * (1 - fetches))

    def rows_of(row, side):
        return pl.ds(pl.multiple_of((2 * row + side) * SHARD, 32), SHARD)

    def piece(part, row, side):
        start = (2 * row + core) * SHARD + side * (SHARD // 2)
        return weights.at[part, pl.ds(pl.multiple_of(start, 16), SHARD // 2)]

    def remote(ref, device, sent, received):
        return pltpu.make_async_remote_copy(
            src_ref=ref,
            dst_ref=ref,
            send_sem=sent,
            recv_sem=received,
            device_id=device,
            device_id_type=MESH,
        )

    def along(part, row, device, index):
        return remote(
            piece(part, row, half), device, y_send.at[part, index], piece_recv.at[part, row]
        )

    def aside(part, row, index):
        return remote(
            piece(part, row, half), beside, x_send.at[part, index], cross_recv.at[part, row]
        )

    def to_mate(part, row, index):
        ref = weights.at[part, rows_of(row, core)]
        return remote(ref, mate, mate_send.at[part, index], mate_recv.at[part, row])

    def z_copies(part):
        sign = 1 - 2 * (z_low // 3)
        return [
            remote(
                piece(part, y, half),
                (partner, ctx + distance * sign),
                z_send.at[part, index],
                piece_recv.at[part, y],
            )
            for index, distance in enumerate((16, 24))
        ]

    def ring_copies(part):
        return [along(part, y, up, 0), along(part, y, down, 1), along(part, y, opposite, 2)]

    def owner(part, action):
        @pl.when(fetches == 0)
        def _():
            @pl.when(border == 1)
            def _():
                for copy in z_copies(part):
                    action(copy)

            for copy in ring_copies(part):
                action(copy)

    def start(copy):
        copy.start()

    def open_part(part):
        owner(part, start)

    def relay(part):
        @pl.when(fetches == 1)
        def _():
            along(part, y, up, 0).wait_recv()
            for copy in ring_copies(part):
                copy.start()
            aside(part, y, 0).start()

    def collect(part):
        for index, row in enumerate((below, above, across)):
            along(part, row, up, 0).wait_recv()
            aside(part, row, index + 1).start()

    def share(part):
        @pl.when(fetches == 1)
        def _():
            remote(
                piece(part, y, 1 - half), beside, x_send.at[part, 0], cross_recv.at[part, y]
            ).wait_recv()
            to_mate(part, y, 0).start()

        for index, row in enumerate((below, above, across)):
            remote(
                piece(part, row, 1 - half), beside, x_send.at[part, 0], cross_recv.at[part, row]
            ).wait_recv()
            to_mate(part, row, index + 1).start()

    def complete(part):
        def finish(row):
            ref = weights.at[part, rows_of(row, 1 - core)]
            remote(ref, mate, mate_send.at[part, 0], mate_recv.at[part, row]).wait_recv()

        @pl.when(fetches == 0)
        def _():
            finish(y)

        for row in (below, above, across):
            finish(row)

    halos = []

    def halo(source, target, device):
        index = len(halos)
        copy = pltpu.make_async_remote_copy(
            src_ref=source,
            dst_ref=target,
            send_sem=halo_send.at[index],
            recv_sem=halo_recv.at[index],
            device_id=device,
            device_id_type=MESH,
        )
        copy.start()
        halos.append(copy)

    open_part(0)
    for copy in last_loads:
        copy.wait()
    dequantise(1)
    dequantise(2)
    letter_load.wait()
    halo(letters.at[:, pl.ds(ROWS - 256, 256)], token_forward, after)
    halo(letters.at[:, pl.ds(0, 256)], token_backward, before)
    halo(hidden.at[pl.ds(ROWS - HALO, HALO), pl.ds(0, WIDTH)], halo_forward, after)
    halo(hidden.at[pl.ds(0, HALO), pl.ds(WIDTH, WIDTH)], halo_backward, before)
    for copy in filter_loads:
        copy.wait()
    short = short_filter[...].astype(F32)
    long = long_filter[...]
    padded = jnp.concatenate([short, jnp.zeros((16 - SHORT, WIDTH), F32)], axis=0).astype(BF16)
    dot = functools.partial(jnp.dot, preferred_element_type=F32)
    long_hat = dot(long_high[...], long) + dot(long_low[...], long)
    short_hat = dot(short_high[...], padded) + dot(short_low[...], padded)
    real_long, imag_long = long_hat[:BLOCK], long_hat[BLOCK:]
    real_short, imag_short = short_hat[:BLOCK], short_hat[BLOCK:]
    first = lax.broadcasted_iota(jnp.int32, (BLOCK, WIDTH), 0) == 0
    scale = jnp.where(first, 1.0 / SPAN, 2.0 / SPAN)
    reals, imags = real_short * real_long, imag_short * imag_long
    pure[...] = jnp.where(first, reals, reals - imags) * scale
    edge[...] = jnp.where(first, imags, reals - imags) * scale
    cross[...] = jnp.where(first, 0.0, real_short * imag_long + imag_short * real_long) * scale
    long_head = long[:16].astype(F32)
    taps[0:1] = short[0:1] * long_head[0:1]
    taps[1:2] = short[0:1] * long_head[1:2] + short[1:2] * long_head[0:1]

    relay(0)
    open_part(1)
    open_part(2)

    def keep_rows(values, live):
        flags = jnp.where(values != 4, live, 0.0)
        return jnp.transpose(jnp.broadcast_to(flags, (128, 128)))

    one = jnp.float32(1.0)
    for block in range(ROWS // 128):
        keep[block * 128 + 256 : block * 128 + 384] = keep_rows(
            letters[:, block * 128 : block * 128 + 128], one
        )

    def project(values):
        wide = values.astype(F32)
        mean = jnp.mean(wide * wide, axis=-1, keepdims=True)
        return (wide * lax.rsqrt(mean + 1e-5)).astype(BF16)

    for copy in state_loads:
        copy.wait()

    def norm_pass(tile, carry):
        rows = pl.ds(pl.multiple_of(tile * TILE, TILE), TILE)
        for strand in range(2):
            normed[strand, rows] = project(state[strand, rows])
        return carry

    lax.fori_loop(0, 2, norm_pass, 0)
    collect(0)
    relay(1)
    relay(2)
    lax.fori_loop(2, ROWS // TILE, norm_pass, 0)
    for copy in table_loads:
        copy.wait()
    share(0)
    collect(1)
    complete(0)

    def value_part(norm, flags):
        return (dot(norm, weights[0]) * jnp.tile(flags, (1, 6))).astype(BF16)

    def value_pass(tile, carry):
        start = pl.multiple_of(tile * TILE, TILE)
        rows = pl.ds(start, TILE)
        flags = keep[pl.ds(start + 256, TILE)]
        masked_forward[pl.ds(pl.multiple_of(start + HALO, 16), TILE)] = value_part(
            normed[0, rows], flags
        )
        masked_backward[rows] = value_part(normed[1, rows], flags)
        return carry

    lax.fori_loop(0, 2, value_pass, 0)
    collect(2)
    share(1)
    lax.fori_loop(2, ROWS // TILE, value_pass, 0)

    for copy in halos:
        copy.wait_recv()
    live_before = jnp.where(ctx > 0, 1.0, 0.0)
    live_after = jnp.where(ctx < CTX - 1, 1.0, 0.0)
    for block in range(2):
        columns = slice(block * 128, block * 128 + 128)
        keep[columns] = keep_rows(token_forward[:, columns], live_before)
        keep[ROWS + 256 + block * 128 : ROWS + 384 + block * 128] = keep_rows(
            token_backward[:, columns], live_after
        )
    masked_forward[0:HALO] = value_part(project(halo_forward[...]), keep[256 - HALO : 256])
    masked_backward[ROWS : ROWS + HALO] = value_part(
        project(halo_backward[...]), keep[ROWS + 256 : ROWS + 256 + HALO]
    )
    share(2)
    complete(1)

    def filtered(strand, start, target):
        masked = masked_backward if strand else masked_forward
        origin = start if strand else pl.multiple_of(start + 16, 16)
        window = masked[pl.ds(origin, SPAN)]
        waves = dot(spread[...], window)
        real, imag = waves[:BLOCK], waves[BLOCK:]
        straight, turned = real * pure[...], imag * cross[...]
        upright, bent = imag * edge[...], real * cross[...]
        if strand:
            parts = [straight + turned, upright - bent]
        else:
            parts = [straight - turned, upright + bent]
        product = jnp.concatenate([part.astype(BF16) for part in parts], axis=0)
        gather = gather_backward if strand else gather_forward
        conv[target : target + BLOCK] = dot(gather[...], product)
        last, second = taps[0:1], taps[1:2]
        row = lax.broadcasted_iota(jnp.int32, (8, WIDTH), 0)
        if strand:
            wrong = masked[pl.ds(start, 16)].astype(F32)
            right = masked[pl.ds(pl.multiple_of(start + SPAN, 16), 16)].astype(F32)
            gap = right - wrong
            outer, inner = gap[0:1], gap[1:2]
            fix = jnp.where(row == 7, second * outer + last * inner, 0.0)
            fix = fix + jnp.where(row == 6, last * outer, 0.0)
            conv[target + BLOCK - 8 : target + BLOCK] += fix
        else:
            right = masked[pl.ds(start, 16)].astype(F32)
            wrong = masked[pl.ds(pl.multiple_of(start + SPAN, 16), 16)].astype(F32)
            gap = right - wrong
            outer, inner = gap[15:16], gap[14:15]
            fix = jnp.where(row == 0, second * outer + last * inner, 0.0)
            fix = fix + jnp.where(row == 1, last * outer, 0.0)
            conv[target : target + 8] += fix

    def gate_pass(tile, carry):
        start = pl.multiple_of(tile * TILE, TILE)
        rows = pl.ds(start, TILE)
        for strand in range(2):
            base = strand * TILE
            for block in range(TILE // BLOCK):
                filtered(strand, pl.multiple_of(start + block * BLOCK, BLOCK), base + block * BLOCK)
            gate = dot(normed[strand, rows], weights[1])
            half_gate = 0.5 * gate
            gated = (half_gate * jnp.tanh(half_gate) + half_gate) * conv[base : base + TILE]
            normed[strand, rows] = gated.astype(BF16)
        return carry

    lax.fori_loop(0, ROWS // TILE, gate_pass, 0)
    complete(2)

    def store(strand, start):
        rows = pl.ds(start, TILE)
        columns = pl.ds(strand * WIDTH, WIDTH)
        return pltpu.make_async_copy(
            state.at[strand, rows], out.at[rows, columns], store_sem.at[strand, start // TILE]
        )

    def out_pass(tile, carry):
        start = pl.multiple_of(tile * TILE, TILE)
        rows = pl.ds(start, TILE)
        for strand in range(2):
            branch = dot(normed[strand, rows], weights[2])
            state[strand, rows] = (state[strand, rows].astype(F32) + branch).astype(BF16)
            store(strand, start).start()
        return carry

    lax.fori_loop(0, ROWS // TILE, out_pass, 0)

    for copy in halos:
        copy.wait_send()
    for part in range(3):
        owner(part, lambda copy: copy.wait_send())

        @pl.when(fetches == 1)
        def _(part=part):
            for copy in ring_copies(part):
                copy.wait_send()
            aside(part, y, 0).wait_send()
            to_mate(part, y, 0).wait_send()

        for index, row in enumerate((below, above, across)):
            aside(part, row, index + 1).wait_send()
            to_mate(part, row, index + 1).wait_send()
    for strand in range(2):
        for tile in range(ROWS // TILE):
            store(strand, tile * TILE).wait()


def shards(
    hidden_state, tokens, in_codes, in_scales, out_codes, out_scales, short_filter, long_filter
):
    anywhere = pl.BlockSpec(memory_space=pl.ANY)
    dma = pltpu.SemaphoreType.DMA
    tables = constants()
    result = pl.pallas_call(
        layer_kernel,
        out_shape=jax.ShapeDtypeStruct((ROWS, 2 * WIDTH), BF16),
        in_specs=[anywhere] * (8 + len(tables)),
        out_specs=anywhere,
        scratch_shapes=[
            pltpu.VMEM((3, WIDTH, WIDTH), BF16),
            pltpu.VMEM((3, 32, 2 * WIDTH), BF16),
            pltpu.VMEM((3, 32, WIDTH), BF16),
            pltpu.VMEM((3, 12), F32),
            pltpu.VMEM((3, 6), F32),
            pltpu.VMEM((1, ROWS), jnp.int32),
            pltpu.VMEM((1, 256), jnp.int32),
            pltpu.VMEM((1, 256), jnp.int32),
            pltpu.VMEM((HALO, WIDTH), BF16),
            pltpu.VMEM((HALO, WIDTH), BF16),
            pltpu.VMEM((SHORT, WIDTH), BF16),
            pltpu.VMEM((LONG, WIDTH), BF16),
            *(pltpu.VMEM(table.shape, BF16) for table in tables),
            pltpu.VMEM((2, ROWS, WIDTH), BF16),
            pltpu.VMEM((2, ROWS, WIDTH), BF16),
            pltpu.VMEM((ROWS + HALO, WIDTH), BF16),
            pltpu.VMEM((ROWS + HALO, WIDTH), BF16),
            pltpu.VMEM((ROWS + 512, 128), F32),
            pltpu.VMEM((BLOCK, WIDTH), F32),
            pltpu.VMEM((BLOCK, WIDTH), F32),
            pltpu.VMEM((BLOCK, WIDTH), F32),
            pltpu.VMEM((8, WIDTH), F32),
            pltpu.VMEM((2 * TILE, WIDTH), F32),
            dma((16,)),
            dma((2, ROWS // TILE)),
            dma((3, 4)),
            dma((3, 4)),
            dma((3, 4)),
            dma((4,)),
            dma((3, 2)),
            dma((3, 3)),
            dma((3, 4)),
            dma((3, 4)),
            dma((4,)),
        ],
        compiler_params=pltpu.CompilerParams(
            collective_id=0, has_side_effects=True, vmem_limit_bytes=VMEM_LIMIT
        ),
        name="layer",
    )(
        hidden_state[0],
        tokens,
        in_codes,
        in_scales,
        out_codes,
        out_scales,
        short_filter,
        long_filter,
        *map(jnp.asarray, tables),
    )
    return result[None]


def solution(mesh):
    in_specs = (
        P("dp", "ctx", None),
        P("dp", "ctx"),
        P("dp", None, None),
        P("dp", None),
        P("dp", None, None),
        P("dp", None),
        P(),
        P(),
    )
    out_specs = P("dp", "ctx", None)
    return jax.shard_map(shards, mesh=mesh, in_specs=in_specs, out_specs=out_specs, check_vma=False)
```

time: 448 us -> 46.3 us (0.10)
  blocking collectives: 165 us -> 0 us
  matrix products: 85.5 us -> 0 us
  local copies, waits for them, and re-layouts: 62.6 us -> 3.76 us
  waiting for transfers between devices: 58.5 us -> 0 us
  Pallas kernels: 0 us -> 42.4 us
  starting transfers between devices: 33.9 us -> 0 us
  other arithmetic: 27.6 us -> 0 us
  between operations: 13.8 us -> 0.01 us
    all_to_all x2 -> x0, blocking collectives: 90 us -> none  [the longest x1 47 us: mirror_outward(): lax.all_to_all(strand_out, 'ctx', split_axis=0, concat_axis=0, tiled=True)]
    conv_general_dilated x2 -> x0, matrix products: 75.4 us -> none  [depthwise(): lax.conv_general_dilated(values, filter_taps[:, None, :], (1,), 'VALID',...]
    all_gather x2 -> x0, blocking collectives: 74.9 us -> none  [the longest x1 48.3 us: shards(): lax.all_gather(in_scales.astype(jnp.bfloat16), 'dp', axis=0, tiled=True)]
    all_to_all x4 -> x0, waiting for transfers between devices: 54.7 us -> none  [the longest x1 41 us: mirror_inward(): lax.all_to_all(backward_half, 'ctx', split_axis=0, concat_axis=0, tiled=T...]
    pallas_call x0 -> x1, Pallas kernels: none -> 42.4 us  [shards(): pl.pallas_call(layer_kernel, out_shape=jax.ShapeDtypeStruct((ROWS, 2 * WI...]
    rev x5 -> x0, local copies, waits for them, and re-layouts: 30.7 us -> none  [the longest x1 15.3 us: mirror_inward(): first_vals[::-1]]
    all_to_all x4 -> x0, starting transfers between devices: 24.3 us -> none  [the longest x1 10 us: mirror_inward(): lax.all_to_all(letters, 'ctx', split_axis=0, concat_axis=0, tiled=True)]
    conv_general_dilated x4 -> x0, local copies, waits for them, and re-layouts: 17.4 us -> none  [depthwise(): lax.conv_general_dilated(values, filter_taps[:, None, :], (1,), 'VALID',...]
  transfers between devices with their start and end apart: 7 -> 0, of which waited for: 4 -> 0; matrix products, arithmetic and copies ran while one was open for 8% -> 0% of each run, Pallas kernels for 0% -> 0%
where the time goes in v1:
time: 46.3 us; the launch traced here: 46.2 us
  Pallas kernels  42.4 us (92%)
  local copies, waits for them, and re-layouts  3.76 us (8%)
    pallas_call x1, Pallas kernels, shards(): pl.pallas_call(layer_kernel, out_shape=jax.ShapeDtypeStruct((ROWS, 2 * WI...  42.4 us
    unnamed x1, local copies, waits for them, and re-layouts  3.76 us

profile of v1, /device:TPU:1, one launch (start us, length us, event | category | flops | bytes accessed | tf_op | source)
XLA Modules:
  0.0 46.2 jit_solution(7097984176564176371)
XLA Ops:
  0.0 42.4 %layer.1 = bf16[1024,1536]{1,0:T(8,128)(2,1)} custom-call(bf16[1024,1536]{1,0:T(8,128)(2,1)} %bitcast.3, s32[1,1024]{1,0:T(1,128)} %tokens.1, bf16[3,32,1536]{2,1,0:T(8,128)(2,1)} %in_codes.1, f32[3,12]{1,0:T(4,128)} %in_scales.1, bf16[3,32,768]{2,1,0:T(8,128)(2,1)} %out_codes.1, f32[3,6]{1,0:T(4,128)} %out_scales.1, bf16[4,768]{1,0:T(4,128)(2,1)} %short_source.1, ...), custom_call_target="tpu_custom_call" | custom-call | tf_op jit(solution)/shard_map/layer/pallas_call | solution.py:503
  42.4 3.8 %copy.17 = bf16[1,1024,1536]{2,1,0:T(8,128)(2,1)} copy(bf16[1,1024,1536]{2,1,0:T(8,128)(2,1)} %bitcast.2) | data formatting | bytes 6291456

commit v2 on v1

--- a/solution.py
+++ b/solution.py
@@ -13,7 +13,7 @@
 ROWS, HALO = 1024, 144
 WIDTH, SHARD = 768, 96
 BLOCK, SPAN = 128, 256
-TILE = 256
+TILE, PART = 512, 256
 DP, CTX = 8, 32
 LONG, SHORT = 128, 4
 VMEM_LIMIT = 63 << 20
@@ -68,7 +68,8 @@
     long_low_source,
     short_high_source,
     short_low_source,
-    out,
+    gated_out,
+    last_weights,
     weights,
     codes,
     last_codes,
@@ -127,6 +128,16 @@
     border = z_low // 3 + (3 - z_low) // 3
     fetches = (core + z_high) % 2
 
+    barrier = pltpu.get_barrier_semaphore()
+    for device in (up, down, opposite, beside_source, mate, after, before):
+        pl.semaphore_signal(barrier, inc=1, device_id=device, device_id_type=MESH)
+
+    @pl.when(fetches == 1)
+    def _():
+        shift = (z_low // 2) * 24
+        source = (partner, ctx + 24 - 8 * z_low - shift)
+        pl.semaphore_signal(barrier, inc=1, device_id=source, device_id_type=MESH)
+
     loads = []
 
     def load(source, target):
@@ -156,16 +167,6 @@
         load(gather_backward_source, gather_backward),
     ]
 
-    barrier = pltpu.get_barrier_semaphore()
-    for device in (up, down, opposite, beside_source, mate, after, before):
-        pl.semaphore_signal(barrier, inc=1, device_id=device, device_id_type=MESH)
-
-    @pl.when(fetches == 1)
-    def _():
-        shift = (z_low // 2) * 24
-        source = (partner, ctx + 24 - 8 * z_low - shift)
-        pl.semaphore_signal(barrier, inc=1, device_id=source, device_id_type=MESH)
-
     def dequantise(part):
         for block in range(3):
             rows = pl.ds(pl.multiple_of(dp * SHARD + block * 32, 32), 32)
@@ -306,12 +307,49 @@
     for copy in last_loads:
         copy.wait()
     dequantise(1)
+    open_part(1)
     dequantise(2)
+    open_part(2)
     letter_load.wait()
     halo(letters.at[:, pl.ds(ROWS - 256, 256)], token_forward, after)
     halo(letters.at[:, pl.ds(0, 256)], token_backward, before)
     halo(hidden.at[pl.ds(ROWS - HALO, HALO), pl.ds(0, WIDTH)], halo_forward, after)
     halo(hidden.at[pl.ds(0, HALO), pl.ds(WIDTH, WIDTH)], halo_backward, before)
+
+    def keep_rows(values, live):
+        flags = jnp.where(values != 4, live, 0.0)
+        return jnp.transpose(jnp.broadcast_to(flags, (128, 128)))
+
+    one = jnp.float32(1.0)
+    for block in range(ROWS // 128):
+        keep[block * 128 + 256 : block * 128 + 384] = keep_rows(
+            letters[:, block * 128 : block * 128 + 128], one
+        )
+
+    def project(values):
+        wide = values.astype(F32)
+        mean = jnp.mean(wide * wide, axis=-1, keepdims=True)
+        return (wide * lax.rsqrt(mean + 1e-5)).astype(BF16)
+
+    for copy in state_loads:
+        copy.wait()
+
+    def norm_pass(part, carry):
+        rows = pl.ds(pl.multiple_of(part * PART, PART), PART)
+        for strand in range(2):
+            start = part // 2 * (2 * TILE) + strand * TILE + part % 2 * PART
+            normed[pl.ds(pl.multiple_of(start, PART), PART)] = project(state[strand, rows])
+        return carry
+
+    lax.fori_loop(0, 1, norm_pass, 0)
+    relay(0)
+    lax.fori_loop(1, 3, norm_pass, 0)
+    relay(1)
+    lax.fori_loop(3, 4, norm_pass, 0)
+    relay(2)
+    collect(0)
+    collect(1)
+
     for copy in filter_loads:
         copy.wait()
     short = short_filter[...].astype(F32)
@@ -332,43 +370,10 @@
     taps[0:1] = short[0:1] * long_head[0:1]
     taps[1:2] = short[0:1] * long_head[1:2] + short[1:2] * long_head[0:1]
 
-    relay(0)
-    open_part(1)
-    open_part(2)
-
-    def keep_rows(values, live):
-        flags = jnp.where(values != 4, live, 0.0)
-        return jnp.transpose(jnp.broadcast_to(flags, (128, 128)))
-
-    one = jnp.float32(1.0)
-    for block in range(ROWS // 128):
-        keep[block * 128 + 256 : block * 128 + 384] = keep_rows(
-            letters[:, block * 128 : block * 128 + 128], one
-        )
-
-    def project(values):
-        wide = values.astype(F32)
-        mean = jnp.mean(wide * wide, axis=-1, keepdims=True)
-        return (wide * lax.rsqrt(mean + 1e-5)).astype(BF16)
-
-    for copy in state_loads:
-        copy.wait()
-
-    def norm_pass(tile, carry):
-        rows = pl.ds(pl.multiple_of(tile * TILE, TILE), TILE)
-        for strand in range(2):
-            normed[strand, rows] = project(state[strand, rows])
-        return carry
-
-    lax.fori_loop(0, 2, norm_pass, 0)
-    collect(0)
-    relay(1)
-    relay(2)
-    lax.fori_loop(2, ROWS // TILE, norm_pass, 0)
     for copy in table_loads:
         copy.wait()
     share(0)
-    collect(1)
+    collect(2)
     complete(0)
 
     def value_part(norm, flags):
@@ -376,18 +381,18 @@
 
     def value_pass(tile, carry):
         start = pl.multiple_of(tile * TILE, TILE)
-        rows = pl.ds(start, TILE)
-        flags = keep[pl.ds(start + 256, TILE)]
-        masked_forward[pl.ds(pl.multiple_of(start + HALO, 16), TILE)] = value_part(
-            normed[0, rows], flags
-        )
-        masked_backward[rows] = value_part(normed[1, rows], flags)
+        values = dot(normed[pl.ds(pl.multiple_of(tile * 2 * TILE, TILE), 2 * TILE)], weights[0])
+        flags = jnp.tile(keep[pl.ds(start + 256, TILE)], (1, 6))
+        masked_forward[pl.ds(pl.multiple_of(start + HALO, 16), TILE)] = (
+            values[:TILE] * flags
+        ).astype(BF16)
+        masked_backward[pl.ds(start, TILE)] = (values[TILE:] * flags).astype(BF16)
         return carry
 
-    lax.fori_loop(0, 2, value_pass, 0)
-    collect(2)
+    lax.fori_loop(0, 1, value_pass, 0)
     share(1)
-    lax.fori_loop(2, ROWS // TILE, value_pass, 0)
+    share(2)
+    lax.fori_loop(1, ROWS // TILE, value_pass, 0)
 
     for copy in halos:
         copy.wait_recv()
@@ -403,7 +408,6 @@
     masked_backward[ROWS : ROWS + HALO] = value_part(
         project(halo_backward[...]), keep[ROWS + 256 : ROWS + 256 + HALO]
     )
-    share(2)
     complete(1)
 
     def filtered(strand, start, target):
@@ -440,39 +444,31 @@
             fix = fix + jnp.where(row == 1, last * outer, 0.0)
             conv[target : target + 8] += fix
 
+    def store(tile):
+        rows = pl.ds(pl.multiple_of(tile * 2 * TILE, TILE), 2 * TILE)
+        return pltpu.make_async_copy(normed.at[rows], gated_out.at[rows], store_sem.at[tile])
+
     def gate_pass(tile, carry):
         start = pl.multiple_of(tile * TILE, TILE)
-        rows = pl.ds(start, TILE)
+        rows = pl.ds(pl.multiple_of(tile * 2 * TILE, TILE), 2 * TILE)
         for strand in range(2):
-            base = strand * TILE
             for block in range(TILE // BLOCK):
-                filtered(strand, pl.multiple_of(start + block * BLOCK, BLOCK), base + block * BLOCK)
-            gate = dot(normed[strand, rows], weights[1])
-            half_gate = 0.5 * gate
-            gated = (half_gate * jnp.tanh(half_gate) + half_gate) * conv[base : base + TILE]
-            normed[strand, rows] = gated.astype(BF16)
+                filtered(
+                    strand,
+                    pl.multiple_of(start + block * BLOCK, BLOCK),
+                    strand * TILE + block * BLOCK,
+                )
+        half_gate = 0.5 * dot(normed[rows], weights[1])
+        gated = (half_gate * jnp.tanh(half_gate) + half_gate) * conv[...]
+        normed[rows] = gated.astype(BF16)
+        store(tile).start()
         return carry
 
-    lax.fori_loop(0, ROWS // TILE, gate_pass, 0)
+    lax.fori_loop(0, ROWS // TILE - 1, gate_pass, 0)
     complete(2)
-
-    def store(strand, start):
-        rows = pl.ds(start, TILE)
-        columns = pl.ds(strand * WIDTH, WIDTH)
-        return pltpu.make_async_copy(
-            state.at[strand, rows], out.at[rows, columns], store_sem.at[strand, start // TILE]
-        )
-
-    def out_pass(tile, carry):
-        start = pl.multiple_of(tile * TILE, TILE)
-        rows = pl.ds(start, TILE)
-        for strand in range(2):
-            branch = dot(normed[strand, rows], weights[2])
-            state[strand, rows] = (state[strand, rows].astype(F32) + branch).astype(BF16)
-            store(strand, start).start()
-        return carry
-
-    lax.fori_loop(0, ROWS // TILE, out_pass, 0)
+    last_store = pltpu.make_async_copy(weights.at[2], last_weights, store_sem.at[ROWS // TILE])
+    last_store.start()
+    lax.fori_loop(ROWS // TILE - 1, ROWS // TILE, gate_pass, 0)
 
     for copy in halos:
         copy.wait_send()
@@ -489,22 +485,62 @@
         for index, row in enumerate((below, above, across)):
             aside(part, row, index + 1).wait_send()
             to_mate(part, row, index + 1).wait_send()
-    for strand in range(2):
-        for tile in range(ROWS // TILE):
-            store(strand, tile * TILE).wait()
+    for tile in range(ROWS // TILE):
+        store(tile).wait()
+    last_store.wait()
+
+
+def finish_kernel(
+    hidden, gated_source, weight_source, out, weight, gated, state, load_sem, ready_sem, store_sem
+):
+    def fetch(unit):
+        rows = pl.ds(pl.multiple_of(unit // 2 * TILE, TILE), TILE)
+        columns = pl.ds(pl.multiple_of(unit % 2 * WIDTH, 128), WIDTH)
+        own = pl.ds(pl.multiple_of(unit * TILE, TILE), TILE)
+        return (
+            pltpu.make_async_copy(gated_source.at[own], gated.at[own], load_sem.at[unit]),
+            pltpu.make_async_copy(hidden.at[rows, columns], state.at[own], ready_sem.at[unit]),
+            pltpu.make_async_copy(state.at[own], out.at[rows, columns], store_sem.at[unit]),
+        )
+
+    units = 2 * ROWS // TILE
+    first = pltpu.make_async_copy(weight_source, weight, load_sem.at[units])
+    first.start()
+    for unit in range(units):
+        for copy in fetch(unit)[:2]:
+            copy.start()
+    first.wait()
+
+    def out_pass(unit, carry):
+        own = pl.ds(pl.multiple_of(unit * TILE, TILE), TILE)
+        *loads, store = fetch(unit)
+        for copy in loads:
+            copy.wait()
+        branch = jnp.dot(gated[own], weight[...], preferred_element_type=F32)
+        state[own] = (state[own].astype(F32) + branch).astype(BF16)
+        store.start()
+        return carry
+
+    lax.fori_loop(0, units, out_pass, 0)
+    for unit in range(units):
+        fetch(unit)[2].wait()
 
 
 def shards(
     hidden_state, tokens, in_codes, in_scales, out_codes, out_scales, short_filter, long_filter
 ):
+    window = hidden_state[0]
     anywhere = pl.BlockSpec(memory_space=pl.ANY)
     dma = pltpu.SemaphoreType.DMA
     tables = constants()
-    result = pl.pallas_call(
+    gated, last_weights = pl.pallas_call(
         layer_kernel,
-        out_shape=jax.ShapeDtypeStruct((ROWS, 2 * WIDTH), BF16),
+        out_shape=(
+            jax.ShapeDtypeStruct((2 * ROWS, WIDTH), BF16),
+            jax.ShapeDtypeStruct((WIDTH, WIDTH), BF16),
+        ),
         in_specs=[anywhere] * (8 + len(tables)),
-        out_specs=anywhere,
+        out_specs=(anywhere, anywhere),
         scratch_shapes=[
             pltpu.VMEM((3, WIDTH, WIDTH), BF16),
             pltpu.VMEM((3, 32, 2 * WIDTH), BF16),
@@ -520,7 +556,7 @@
             pltpu.VMEM((LONG, WIDTH), BF16),
             *(pltpu.VMEM(table.shape, BF16) for table in tables),
             pltpu.VMEM((2, ROWS, WIDTH), BF16),
-            pltpu.VMEM((2, ROWS, WIDTH), BF16),
+            pltpu.VMEM((2 * ROWS, WIDTH), BF16),
             pltpu.VMEM((ROWS + HALO, WIDTH), BF16),
             pltpu.VMEM((ROWS + HALO, WIDTH), BF16),
             pltpu.VMEM((ROWS + 512, 128), F32),
@@ -530,7 +566,7 @@
             pltpu.VMEM((8, WIDTH), F32),
             pltpu.VMEM((2 * TILE, WIDTH), F32),
             dma((16,)),
-            dma((2, ROWS // TILE)),
+            dma((4,)),
             dma((3, 4)),
             dma((3, 4)),
             dma((3, 4)),
@@ -546,7 +582,7 @@
         ),
         name="layer",
     )(
-        hidden_state[0],
+        window,
         tokens,
         in_codes,
         in_scales,
@@ -556,6 +592,22 @@
         long_filter,
         *map(jnp.asarray, tables),
     )
+    result = pl.pallas_call(
+        finish_kernel,
+        out_shape=jax.ShapeDtypeStruct((ROWS, 2 * WIDTH), BF16),
+        in_specs=[anywhere] * 3,
+        out_specs=anywhere,
+        scratch_shapes=[
+            pltpu.VMEM((WIDTH, WIDTH), BF16),
+            pltpu.VMEM((2 * ROWS, WIDTH), BF16),
+            pltpu.VMEM((2 * ROWS, WIDTH), BF16),
+            dma((8,)),
+            dma((8,)),
+            dma((8,)),
+        ],
+        compiler_params=pltpu.CompilerParams(vmem_limit_bytes=VMEM_LIMIT),
+        name="finish",
+    )(window, gated, last_weights)
     return result[None]
 
 

time: 46.3 us -> 45.1 us (0.974)
  local copies, waits for them, and re-layouts: 3.76 us -> 0 us
  Pallas kernels: 42.4 us -> 45.1 us
    unnamed x1 -> x0, local copies, waits for them, and re-layouts: 3.76 us -> none
    pallas_call x1 -> x2, Pallas kernels: 42.4 us -> 45.1 us  [the longest x1 39.1 us: shards(): pl.pallas_call(layer_kernel, out_shape=(jax.ShapeDtypeStruct((2 * ROWS, W...]
where the time goes in v2:
time: 45.1 us
  Pallas kernels  45.1 us (100%)
    pallas_call x1, Pallas kernels, shards(): pl.pallas_call(layer_kernel, out_shape=(jax.ShapeDtypeStruct((2 * ROWS, W...  39.1 us
    pallas_call x1, Pallas kernels, shards(): pl.pallas_call(finish_kernel, out_shape=jax.ShapeDtypeStruct((ROWS, 2 * W...  5.96 us

profile of v2, /device:TPU:1, one launch (start us, length us, event | category | flops | bytes accessed | tf_op | source)
XLA Modules:
  0.0 45.1 jit_solution(15679657536577556238)
XLA Ops:
  0.0 39.1 %layer.1 = (bf16[2048,768]{1,0:T(8,128)(2,1)}, bf16[768,768]{1,0:T(8,128)(2,1)}) custom-call(bf16[1024,1536]{1,0:T(8,128)(2,1)} %bitcast.2, s32[1,1024]{1,0:T(1,128)} %tokens.1, bf16[3,32,1536]{2,1,0:T(8,128)(2,1)} %in_codes.1, f32[3,12]{1,0:T(4,128)} %in_scales.1, bf16[3,32,768]{2,1,0:T(8,128)(2,1)} %out_codes.1, f32[3,6]{1,0:T(4,128)} %out_scales.1, ...), custom_call_target="tpu_custom_call" | custom-call | tf_op jit(solution)/shard_map/layer/pallas_call | solution.py:536
  39.1 6.0 %finish.1 = bf16[1024,1536]{1,0:T(8,128)(2,1)} custom-call(bf16[1024,1536]{1,0:T(8,128)(2,1)} %bitcast.3, bf16[2048,768]{1,0:T(8,128)(2,1)} %get-tuple-element.7.gated_source, bf16[768,768]{1,0:T(8,128)(2,1)} %get-tuple-element.8.weight_source), custom_call_target="tpu_custom_call" | custom-call | tf_op jit(solution)/shard_map/finish/pallas_call | solution.py:595

commit v3 on v2

--- a/solution.py
+++ b/solution.py
@@ -11,9 +11,9 @@
 MESH = pl.DeviceIdType.MESH
 F32, BF16 = jnp.float32, jnp.bfloat16
 ROWS, HALO = 1024, 144
-WIDTH, SHARD = 768, 96
+WIDTH, SHARD, OWN = 768, 96, 384
 BLOCK, SPAN = 128, 256
-TILE, PART = 512, 256
+TILE = 256
 DP, CTX = 8, 32
 LONG, SHORT = 128, 4
 VMEM_LIMIT = 63 << 20
@@ -99,6 +99,8 @@
     edge,
     taps,
     conv,
+    values_sum,
+    gate_sum,
     load_sem,
     store_sem,
     piece_recv,
@@ -121,15 +123,18 @@
     up, down = ((dp + 2) % DP, ctx), ((dp + DP - 2) % DP, ctx)
     opposite = ((dp + 4) % DP, ctx)
     step = 1 - 2 * core
-    beside = (dp, z_low * 8 + (x + ring + step) % ring * 2 + core)
-    beside_source = (dp, z_low * 8 + (x + ring - step) % ring * 2 + core)
+
+    def along_x(distance):
+        return (dp, z_low * 8 + (x + ring + distance) % ring * 2 + core)
+
+    beside = along_x(step)
     mate = (dp, ctx + step)
     after, before = (dp, (ctx + 1) % CTX), (dp, (ctx + CTX - 1) % CTX)
     border = z_low // 3 + (3 - z_low) // 3
     fetches = (core + z_high) % 2
 
     barrier = pltpu.get_barrier_semaphore()
-    for device in (up, down, opposite, beside_source, mate, after, before):
+    for device in (up, down, opposite, along_x(-step), mate, after, before):
         pl.semaphore_signal(barrier, inc=1, device_id=device, device_id_type=MESH)
 
     @pl.when(fetches == 1)
@@ -167,9 +172,15 @@
         load(gather_backward_source, gather_backward),
     ]
 
+    def base_of(part, row, side):
+        if part == 2:
+            return (2 * row + side) * SHARD
+        return (side + z_high) % 2 * OWN + row * SHARD
+
     def dequantise(part):
         for block in range(3):
-            rows = pl.ds(pl.multiple_of(dp * SHARD + block * 32, 32), 32)
+            start = base_of(part, y, z_high) + block * 32
+            rows = pl.ds(pl.multiple_of(start, 32), 32)
             for group in range(6):
                 column = group * 128
                 if part < 2:
@@ -186,17 +197,14 @@
     dequantise(0)
     pl.semaphore_wait(barrier, 7 + 2 * border * (1 - fetches))
 
-    def rows_of(row, side):
-        return pl.ds(pl.multiple_of((2 * row + side) * SHARD, 32), SHARD)
-
-    def piece(part, row, side):
-        start = (2 * row + core) * SHARD + side * (SHARD // 2)
+    def piece(part, row, side, base=None):
+        start = (base_of(part, row, core) if base is None else base) + side * (SHARD // 2)
         return weights.at[part, pl.ds(pl.multiple_of(start, 16), SHARD // 2)]
 
-    def remote(ref, device, sent, received):
+    def remote(ref, device, sent, received, target=None):
         return pltpu.make_async_remote_copy(
             src_ref=ref,
-            dst_ref=ref,
+            dst_ref=ref if target is None else target,
             send_sem=sent,
             recv_sem=received,
             device_id=device,
@@ -210,12 +218,16 @@
 
     def aside(part, row, index):
         return remote(
-            piece(part, row, half), beside, x_send.at[part, index], cross_recv.at[part, row]
-        )
-
-    def to_mate(part, row, index):
-        ref = weights.at[part, rows_of(row, core)]
-        return remote(ref, mate, mate_send.at[part, index], mate_recv.at[part, row])
+            piece(part, row, half),
+            beside,
+            x_send.at[part, index],
+            cross_recv.at[part, row],
+        )
+
+    def to_mate(part, row, side, index):
+        return remote(
+            piece(part, row, side), mate, mate_send.at[part, index], mate_recv.at[part, row]
+        )
 
     def z_copies(part):
         sign = 1 - 2 * (z_low // 3)
@@ -225,6 +237,7 @@
                 (partner, ctx + distance * sign),
                 z_send.at[part, index],
                 piece_recv.at[part, y],
+                piece(part, y, half, None if part == 2 else OWN + y * SHARD),
             )
             for index, distance in enumerate((16, 24))
         ]
@@ -256,37 +269,40 @@
             for copy in ring_copies(part):
                 copy.start()
             aside(part, y, 0).start()
+            to_mate(part, y, half, 0).start()
 
     def collect(part):
         for index, row in enumerate((below, above, across)):
             along(part, row, up, 0).wait_recv()
             aside(part, row, index + 1).start()
+            to_mate(part, row, half, 2 * index + 2).start()
 
     def share(part):
-        @pl.when(fetches == 1)
-        def _():
-            remote(
-                piece(part, y, 1 - half), beside, x_send.at[part, 0], cross_recv.at[part, y]
-            ).wait_recv()
-            to_mate(part, y, 0).start()
-
-        for index, row in enumerate((below, above, across)):
+        def pass_on(row, index):
             remote(
                 piece(part, row, 1 - half), beside, x_send.at[part, 0], cross_recv.at[part, row]
             ).wait_recv()
-            to_mate(part, row, index + 1).start()
-
-    def complete(part):
+            to_mate(part, row, 1 - half, index).start()
+
+        @pl.when(fetches == 1)
+        def _():
+            pass_on(y, 1)
+
+        for index, row in enumerate((below, above, across)):
+            pass_on(row, 2 * index + 3)
+
+    def complete(part, role):
         def finish(row):
-            ref = weights.at[part, rows_of(row, 1 - core)]
+            start = base_of(part, row, 1 - core)
+            ref = weights.at[part, pl.ds(pl.multiple_of(start, 32), SHARD)]
             remote(ref, mate, mate_send.at[part, 0], mate_recv.at[part, row]).wait_recv()
 
-        @pl.when(fetches == 0)
+        @pl.when(fetches == role)
         def _():
-            finish(y)
-
-        for row in (below, above, across):
-            finish(row)
+            if role == 0:
+                finish(y)
+            for row in (below, above, across):
+                finish(row)
 
     halos = []
 
@@ -329,16 +345,26 @@
     def project(values):
         wide = values.astype(F32)
         mean = jnp.mean(wide * wide, axis=-1, keepdims=True)
-        return (wide * lax.rsqrt(mean + 1e-5)).astype(BF16)
+        scaled = wide * lax.rsqrt(mean + 1e-5)
+        low, high = (
+            jnp.concatenate(
+                [scaled[:, start : start + SHARD] for start in range(side * SHARD, WIDTH, 2 * SHARD)],
+                axis=1,
+            )
+            for side in range(2)
+        )
+        own_first = z_high == 0
+        ordered = [jnp.where(own_first, low, high), jnp.where(own_first, high, low)]
+        return jnp.concatenate([item.astype(BF16) for item in ordered], axis=1)
 
     for copy in state_loads:
         copy.wait()
 
-    def norm_pass(part, carry):
-        rows = pl.ds(pl.multiple_of(part * PART, PART), PART)
+    def norm_pass(tile, carry):
+        rows = pl.ds(pl.multiple_of(tile * TILE, TILE), TILE)
         for strand in range(2):
-            start = part // 2 * (2 * TILE) + strand * TILE + part % 2 * PART
-            normed[pl.ds(pl.multiple_of(start, PART), PART)] = project(state[strand, rows])
+            start = (2 * tile + strand) * TILE
+            normed[pl.ds(pl.multiple_of(start, TILE), TILE)] = project(state[strand, rows])
         return carry
 
     lax.fori_loop(0, 1, norm_pass, 0)
@@ -374,14 +400,30 @@
         copy.wait()
     share(0)
     collect(2)
-    complete(0)
+    share(1)
+    complete(0, 1)
+    complete(1, 1)
+
+    def rows_in(tile):
+        return pl.ds(pl.multiple_of(tile * 2 * TILE, TILE), 2 * TILE)
+
+    def own_pass(tile, carry):
+        rows = rows_in(tile)
+        values_sum[rows] = dot(normed[rows, :OWN], weights[0, :OWN])
+        gate_sum[rows] = dot(normed[rows, :OWN], weights[1, :OWN])
+        return carry
+
+    lax.fori_loop(0, ROWS // TILE, own_pass, 0)
+    share(2)
+    complete(0, 0)
 
     def value_part(norm, flags):
         return (dot(norm, weights[0]) * jnp.tile(flags, (1, 6))).astype(BF16)
 
     def value_pass(tile, carry):
         start = pl.multiple_of(tile * TILE, TILE)
-        values = dot(normed[pl.ds(pl.multiple_of(tile * 2 * TILE, TILE), 2 * TILE)], weights[0])
+        rows = rows_in(tile)
+        values = values_sum[rows] + dot(normed[rows, OWN:], weights[0, OWN:])
         flags = jnp.tile(keep[pl.ds(start + 256, TILE)], (1, 6))
         masked_forward[pl.ds(pl.multiple_of(start + HALO, 16), TILE)] = (
             values[:TILE] * flags
@@ -389,10 +431,7 @@
         masked_backward[pl.ds(start, TILE)] = (values[TILE:] * flags).astype(BF16)
         return carry
 
-    lax.fori_loop(0, 1, value_pass, 0)
-    share(1)
-    share(2)
-    lax.fori_loop(1, ROWS // TILE, value_pass, 0)
+    lax.fori_loop(0, ROWS // TILE, value_pass, 0)
 
     for copy in halos:
         copy.wait_recv()
@@ -408,7 +447,7 @@
     masked_backward[ROWS : ROWS + HALO] = value_part(
         project(halo_backward[...]), keep[ROWS + 256 : ROWS + 256 + HALO]
     )
-    complete(1)
+    complete(1, 0)
 
     def filtered(strand, start, target):
         masked = masked_backward if strand else masked_forward
@@ -445,27 +484,26 @@
             conv[target : target + 8] += fix
 
     def store(tile):
-        rows = pl.ds(pl.multiple_of(tile * 2 * TILE, TILE), 2 * TILE)
+        rows = rows_in(tile)
         return pltpu.make_async_copy(normed.at[rows], gated_out.at[rows], store_sem.at[tile])
 
     def gate_pass(tile, carry):
         start = pl.multiple_of(tile * TILE, TILE)
-        rows = pl.ds(pl.multiple_of(tile * 2 * TILE, TILE), 2 * TILE)
+        rows = rows_in(tile)
         for strand in range(2):
             for block in range(TILE // BLOCK):
-                filtered(
-                    strand,
-                    pl.multiple_of(start + block * BLOCK, BLOCK),
-                    strand * TILE + block * BLOCK,
-                )
-        half_gate = 0.5 * dot(normed[rows], weights[1])
+                offset = block * BLOCK
+                filtered(strand, pl.multiple_of(start + offset, BLOCK), strand * TILE + offset)
+        gate = gate_sum[rows] + dot(normed[rows, OWN:], weights[1, OWN:])
+        half_gate = 0.5 * gate
         gated = (half_gate * jnp.tanh(half_gate) + half_gate) * conv[...]
         normed[rows] = gated.astype(BF16)
         store(tile).start()
         return carry
 
-    lax.fori_loop(0, ROWS // TILE - 1, gate_pass, 0)
-    complete(2)
+    lax.fori_loop(0, 3, gate_pass, 0)
+    complete(2, 0)
+    complete(2, 1)
     last_store = pltpu.make_async_copy(weights.at[2], last_weights, store_sem.at[ROWS // TILE])
     last_store.start()
     lax.fori_loop(ROWS // TILE - 1, ROWS // TILE, gate_pass, 0)
@@ -480,11 +518,13 @@
             for copy in ring_copies(part):
                 copy.wait_send()
             aside(part, y, 0).wait_send()
-            to_mate(part, y, 0).wait_send()
+            for side in range(2):
+                to_mate(part, y, side, side).wait_send()
 
         for index, row in enumerate((below, above, across)):
             aside(part, row, index + 1).wait_send()
-            to_mate(part, row, index + 1).wait_send()
+            for side in range(2):
+                to_mate(part, row, side, 2 * index + 2 + side).wait_send()
     for tile in range(ROWS // TILE):
         store(tile).wait()
     last_store.wait()
@@ -494,16 +534,15 @@
     hidden, gated_source, weight_source, out, weight, gated, state, load_sem, ready_sem, store_sem
 ):
     def fetch(unit):
-        rows = pl.ds(pl.multiple_of(unit // 2 * TILE, TILE), TILE)
-        columns = pl.ds(pl.multiple_of(unit % 2 * WIDTH, 128), WIDTH)
-        own = pl.ds(pl.multiple_of(unit * TILE, TILE), TILE)
+        rows = pl.ds(pl.multiple_of(unit * TILE, TILE), TILE)
+        own = pl.ds(pl.multiple_of(unit * 2 * TILE, TILE), 2 * TILE)
         return (
             pltpu.make_async_copy(gated_source.at[own], gated.at[own], load_sem.at[unit]),
-            pltpu.make_async_copy(hidden.at[rows, columns], state.at[own], ready_sem.at[unit]),
-            pltpu.make_async_copy(state.at[own], out.at[rows, columns], store_sem.at[unit]),
-        )
-
-    units = 2 * ROWS // TILE
+            pltpu.make_async_copy(hidden.at[rows], state.at[rows], ready_sem.at[unit]),
+            pltpu.make_async_copy(state.at[rows], out.at[rows], store_sem.at[unit]),
+        )
+
+    units = ROWS // TILE
     first = pltpu.make_async_copy(weight_source, weight, load_sem.at[units])
     first.start()
     for unit in range(units):
@@ -512,12 +551,16 @@
     first.wait()
 
     def out_pass(unit, carry):
-        own = pl.ds(pl.multiple_of(unit * TILE, TILE), TILE)
+        rows = pl.ds(pl.multiple_of(unit * TILE, TILE), TILE)
+        own = pl.ds(pl.multiple_of(unit * 2 * TILE, TILE), 2 * TILE)
         *loads, store = fetch(unit)
         for copy in loads:
             copy.wait()
         branch = jnp.dot(gated[own], weight[...], preferred_element_type=F32)
-        state[own] = (state[own].astype(F32) + branch).astype(BF16)
+        for strand in range(2):
+            columns = slice(strand * WIDTH, strand * WIDTH + WIDTH)
+            added = branch[strand * TILE : strand * TILE + TILE]
+            state[rows, columns] = (state[rows, columns].astype(F32) + added).astype(BF16)
         store.start()
         return carry
 
@@ -565,8 +608,10 @@
             pltpu.VMEM((BLOCK, WIDTH), F32),
             pltpu.VMEM((8, WIDTH), F32),
             pltpu.VMEM((2 * TILE, WIDTH), F32),
+            pltpu.VMEM((2 * ROWS, WIDTH), F32),
+            pltpu.VMEM((2 * ROWS, WIDTH), F32),
             dma((16,)),
-            dma((4,)),
+            dma((8,)),
             dma((3, 4)),
             dma((3, 4)),
             dma((3, 4)),
@@ -574,7 +619,7 @@
             dma((3, 2)),
             dma((3, 3)),
             dma((3, 4)),
-            dma((3, 4)),
+            dma((3, 8)),
             dma((4,)),
         ],
         compiler_params=pltpu.CompilerParams(
@@ -600,7 +645,7 @@
         scratch_shapes=[
             pltpu.VMEM((WIDTH, WIDTH), BF16),
             pltpu.VMEM((2 * ROWS, WIDTH), BF16),
-            pltpu.VMEM((2 * ROWS, WIDTH), BF16),
+            pltpu.VMEM((ROWS, 2 * WIDTH), BF16),
             dma((8,)),
             dma((8,)),
             dma((8,)),

time: 45.1 us -> 46.6 us (1.033)
  Pallas kernels: 45.1 us -> 46.5 us
    pallas_call x1, Pallas kernels: 39.1 us -> 40.6 us  [shards(): pl.pallas_call(layer_kernel, out_shape=(jax.ShapeDtypeStruct((2 * ROWS, W...]
where the time goes in v3:
time: 46.6 us; the launch traced here: 46.5 us
  Pallas kernels  46.5 us (100%)
    pallas_call x1, Pallas kernels, shards(): pl.pallas_call(layer_kernel, out_shape=(jax.ShapeDtypeStruct((2 * ROWS, W...  40.6 us
    pallas_call x1, Pallas kernels, shards(): pl.pallas_call(finish_kernel, out_shape=jax.ShapeDtypeStruct((ROWS, 2 * W...  5.95 us

profile of v3, /device:TPU:1, one launch (start us, length us, event | category | flops | bytes accessed | tf_op | source)
XLA Modules:
  0.0 46.5 jit_solution(11648822786323243194)
XLA Ops:
  0.0 40.6 %layer.1 = (bf16[2048,768]{1,0:T(8,128)(2,1)}, bf16[768,768]{1,0:T(8,128)(2,1)}) custom-call(bf16[1024,1536]{1,0:T(8,128)(2,1)} %bitcast.2, s32[1,1024]{1,0:T(1,128)} %tokens.1, bf16[3,32,1536]{2,1,0:T(8,128)(2,1)} %in_codes.1, f32[3,12]{1,0:T(4,128)} %in_scales.1, bf16[3,32,768]{2,1,0:T(8,128)(2,1)} %out_codes.1, f32[3,6]{1,0:T(4,128)} %out_scales.1, ...), custom_call_target="tpu_custom_call" | custom-call | tf_op jit(solution)/shard_map/layer/pallas_call | solution.py:579
  40.6 6.0 %finish.1 = bf16[1024,1536]{1,0:T(8,128)(2,1)} custom-call(bf16[1024,1536]{1,0:T(8,128)(2,1)} %bitcast.3, bf16[2048,768]{1,0:T(8,128)(2,1)} %get-tuple-element.7.gated_source, bf16[768,768]{1,0:T(8,128)(2,1)} %get-tuple-element.8.weight_source), custom_call_target="tpu_custom_call" | custom-call | tf_op jit(solution)/shard_map/finish/pallas_call | solution.py:640

commit v4 on v3

--- a/solution.py
+++ b/solution.py
@@ -11,7 +11,7 @@
 MESH = pl.DeviceIdType.MESH
 F32, BF16 = jnp.float32, jnp.bfloat16
 ROWS, HALO = 1024, 144
-WIDTH, SHARD, OWN = 768, 96, 384
+WIDTH, SHARD = 768, 96
 BLOCK, SPAN = 128, 256
 TILE = 256
 DP, CTX = 8, 32
@@ -99,8 +99,6 @@
     edge,
     taps,
     conv,
-    values_sum,
-    gate_sum,
     load_sem,
     store_sem,
     piece_recv,
@@ -172,14 +170,12 @@
         load(gather_backward_source, gather_backward),
     ]
 
-    def base_of(part, row, side):
-        if part == 2:
-            return (2 * row + side) * SHARD
-        return (side + z_high) % 2 * OWN + row * SHARD
+    def base_of(row, side):
+        return (2 * row + side) * SHARD
 
     def dequantise(part):
         for block in range(3):
-            start = base_of(part, y, z_high) + block * 32
+            start = base_of(y, z_high) + block * 32
             rows = pl.ds(pl.multiple_of(start, 32), 32)
             for group in range(6):
                 column = group * 128
@@ -197,15 +193,15 @@
     dequantise(0)
     pl.semaphore_wait(barrier, 7 + 2 * border * (1 - fetches))
 
-    def piece(part, row, side, base=None):
-        start = (base_of(part, row, core) if base is None else base) + side * (SHARD // 2)
+    def piece(part, row, side):
+        start = base_of(row, core) + side * (SHARD // 2)
         return weights.at[part, pl.ds(pl.multiple_of(start, 16), SHARD // 2)]
 
-    def remote(ref, device, sent, received, target=None):
+    def remote(ref, device, left, received):
         return pltpu.make_async_remote_copy(
             src_ref=ref,
-            dst_ref=ref if target is None else target,
-            send_sem=sent,
+            dst_ref=ref,
+            send_sem=left,
             recv_sem=received,
             device_id=device,
             device_id_type=MESH,
@@ -237,7 +233,6 @@
                 (partner, ctx + distance * sign),
                 z_send.at[part, index],
                 piece_recv.at[part, y],
-                piece(part, y, half, None if part == 2 else OWN + y * SHARD),
             )
             for index, distance in enumerate((16, 24))
         ]
@@ -245,22 +240,23 @@
     def ring_copies(part):
         return [along(part, y, up, 0), along(part, y, down, 1), along(part, y, opposite, 2)]
 
-    def owner(part, action):
+    def z_owner(part, action):
+        @pl.when(fetches + (1 - border) == 0)
+        def _():
+            for copy in z_copies(part):
+                action(copy)
+
+    def ring_owner(part, action):
         @pl.when(fetches == 0)
         def _():
-            @pl.when(border == 1)
-            def _():
-                for copy in z_copies(part):
-                    action(copy)
-
             for copy in ring_copies(part):
                 action(copy)
 
     def start(copy):
         copy.start()
 
-    def open_part(part):
-        owner(part, start)
+    def sent(copy):
+        copy.wait_send()
 
     def relay(part):
         @pl.when(fetches == 1)
@@ -291,18 +287,17 @@
         for index, row in enumerate((below, above, across)):
             pass_on(row, 2 * index + 3)
 
-    def complete(part, role):
+    def complete(part):
         def finish(row):
-            start = base_of(part, row, 1 - core)
-            ref = weights.at[part, pl.ds(pl.multiple_of(start, 32), SHARD)]
+            ref = weights.at[part, pl.ds(pl.multiple_of(base_of(row, 1 - core), 32), SHARD)]
             remote(ref, mate, mate_send.at[part, 0], mate_recv.at[part, row]).wait_recv()
 
-        @pl.when(fetches == role)
+        @pl.when(fetches == 0)
         def _():
-            if role == 0:
-                finish(y)
-            for row in (below, above, across):
-                finish(row)
+            finish(y)
+
+        for row in (below, above, across):
+            finish(row)
 
     halos = []
 
@@ -319,18 +314,19 @@
         copy.start()
         halos.append(copy)
 
-    open_part(0)
-    for copy in last_loads:
-        copy.wait()
-    dequantise(1)
-    open_part(1)
-    dequantise(2)
-    open_part(2)
+    z_owner(0, start)
+    ring_owner(0, start)
     letter_load.wait()
     halo(letters.at[:, pl.ds(ROWS - 256, 256)], token_forward, after)
     halo(letters.at[:, pl.ds(0, 256)], token_backward, before)
     halo(hidden.at[pl.ds(ROWS - HALO, HALO), pl.ds(0, WIDTH)], halo_forward, after)
     halo(hidden.at[pl.ds(0, HALO), pl.ds(WIDTH, WIDTH)], halo_backward, before)
+    for copy in last_loads:
+        copy.wait()
+    dequantise(1)
+    z_owner(0, sent)
+    z_owner(1, start)
+    dequantise(2)
 
     def keep_rows(values, live):
         flags = jnp.where(values != 4, live, 0.0)
@@ -345,20 +341,7 @@
     def project(values):
         wide = values.astype(F32)
         mean = jnp.mean(wide * wide, axis=-1, keepdims=True)
-        scaled = wide * lax.rsqrt(mean + 1e-5)
-        low, high = (
-            jnp.concatenate(
-                [scaled[:, start : start + SHARD] for start in range(side * SHARD, WIDTH, 2 * SHARD)],
-                axis=1,
-            )
-            for side in range(2)
-        )
-        own_first = z_high == 0
-        ordered = [jnp.where(own_first, low, high), jnp.where(own_first, high, low)]
-        return jnp.concatenate([item.astype(BF16) for item in ordered], axis=1)
-
-    for copy in state_loads:
-        copy.wait()
+        return (wide * lax.rsqrt(mean + 1e-5)).astype(BF16)
 
     def norm_pass(tile, carry):
         rows = pl.ds(pl.multiple_of(tile * TILE, TILE), TILE)
@@ -367,14 +350,23 @@
             normed[pl.ds(pl.multiple_of(start, TILE), TILE)] = project(state[strand, rows])
         return carry
 
+    relay(0)
+    z_owner(1, sent)
+    z_owner(2, start)
+    for copy in state_loads:
+        copy.wait()
     lax.fori_loop(0, 1, norm_pass, 0)
-    relay(0)
-    lax.fori_loop(1, 3, norm_pass, 0)
     relay(1)
-    lax.fori_loop(3, 4, norm_pass, 0)
+    ring_owner(1, start)
+    lax.fori_loop(1, 2, norm_pass, 0)
     relay(2)
     collect(0)
+    ring_owner(2, start)
+    lax.fori_loop(2, 3, norm_pass, 0)
     collect(1)
+    lax.fori_loop(3, 4, norm_pass, 0)
+    collect(2)
+    share(0)
 
     for copy in filter_loads:
         copy.wait()
@@ -398,24 +390,10 @@
 
     for copy in table_loads:
         copy.wait()
-    share(0)
-    collect(2)
-    share(1)
-    complete(0, 1)
-    complete(1, 1)
+    complete(0)
 
     def rows_in(tile):
         return pl.ds(pl.multiple_of(tile * 2 * TILE, TILE), 2 * TILE)
-
-    def own_pass(tile, carry):
-        rows = rows_in(tile)
-        values_sum[rows] = dot(normed[rows, :OWN], weights[0, :OWN])
-        gate_sum[rows] = dot(normed[rows, :OWN], weights[1, :OWN])
-        return carry
-
-    lax.fori_loop(0, ROWS // TILE, own_pass, 0)
-    share(2)
-    complete(0, 0)
 
     def value_part(norm, flags):
         return (dot(norm, weights[0]) * jnp.tile(flags, (1, 6))).astype(BF16)
@@ -423,7 +401,7 @@
     def value_pass(tile, carry):
         start = pl.multiple_of(tile * TILE, TILE)
         rows = rows_in(tile)
-        values = values_sum[rows] + dot(normed[rows, OWN:], weights[0, OWN:])
+        values = dot(normed[rows], weights[0])
         flags = jnp.tile(keep[pl.ds(start + 256, TILE)], (1, 6))
         masked_forward[pl.ds(pl.multiple_of(start + HALO, 16), TILE)] = (
             values[:TILE] * flags
@@ -431,7 +409,10 @@
         masked_backward[pl.ds(start, TILE)] = (values[TILE:] * flags).astype(BF16)
         return carry
 
-    lax.fori_loop(0, ROWS // TILE, value_pass, 0)
+    lax.fori_loop(0, 2, value_pass, 0)
+    share(1)
+    lax.fori_loop(2, ROWS // TILE, value_pass, 0)
+    share(2)
 
     for copy in halos:
         copy.wait_recv()
@@ -447,7 +428,7 @@
     masked_backward[ROWS : ROWS + HALO] = value_part(
         project(halo_backward[...]), keep[ROWS + 256 : ROWS + 256 + HALO]
     )
-    complete(1, 0)
+    complete(1)
 
     def filtered(strand, start, target):
         masked = masked_backward if strand else masked_forward
@@ -494,24 +475,23 @@
             for block in range(TILE // BLOCK):
                 offset = block * BLOCK
                 filtered(strand, pl.multiple_of(start + offset, BLOCK), strand * TILE + offset)
-        gate = gate_sum[rows] + dot(normed[rows, OWN:], weights[1, OWN:])
-        half_gate = 0.5 * gate
+        half_gate = 0.5 * dot(normed[rows], weights[1])
         gated = (half_gate * jnp.tanh(half_gate) + half_gate) * conv[...]
         normed[rows] = gated.astype(BF16)
         store(tile).start()
         return carry
 
     lax.fori_loop(0, 3, gate_pass, 0)
-    complete(2, 0)
-    complete(2, 1)
+    complete(2)
     last_store = pltpu.make_async_copy(weights.at[2], last_weights, store_sem.at[ROWS // TILE])
     last_store.start()
     lax.fori_loop(ROWS // TILE - 1, ROWS // TILE, gate_pass, 0)
 
     for copy in halos:
         copy.wait_send()
+    z_owner(2, sent)
     for part in range(3):
-        owner(part, lambda copy: copy.wait_send())
+        ring_owner(part, sent)
 
         @pl.when(fetches == 1)
         def _(part=part):
@@ -608,8 +588,6 @@
             pltpu.VMEM((BLOCK, WIDTH), F32),
             pltpu.VMEM((8, WIDTH), F32),
             pltpu.VMEM((2 * TILE, WIDTH), F32),
-            pltpu.VMEM((2 * ROWS, WIDTH), F32),
-            pltpu.VMEM((2 * ROWS, WIDTH), F32),
             dma((16,)),
             dma((8,)),
             dma((3, 4)),

time: 46.6 us -> 45.4 us (0.974)
  Pallas kernels: 46.5 us -> 45.4 us
    pallas_call x1, Pallas kernels: 40.6 us -> 39.4 us  [shards(): pl.pallas_call(layer_kernel, out_shape=(jax.ShapeDtypeStruct((2 * ROWS, W...]
where the time goes in v4:
time: 45.4 us
  Pallas kernels  45.4 us (100%)
    pallas_call x1, Pallas kernels, shards(): pl.pallas_call(layer_kernel, out_shape=(jax.ShapeDtypeStruct((2 * ROWS, W...  39.4 us
    pallas_call x1, Pallas kernels, shards(): pl.pallas_call(finish_kernel, out_shape=jax.ShapeDtypeStruct((ROWS, 2 * W...  5.95 us

profile of v4, /device:TPU:1, one launch (start us, length us, event | category | flops | bytes accessed | tf_op | source)
XLA Modules:
  0.0 45.4 jit_solution(1224239210285572926)
XLA Ops:
  0.0 39.4 %layer.1 = (bf16[2048,768]{1,0:T(8,128)(2,1)}, bf16[768,768]{1,0:T(8,128)(2,1)}) custom-call(bf16[1024,1536]{1,0:T(8,128)(2,1)} %bitcast.2, s32[1,1024]{1,0:T(1,128)} %tokens.1, bf16[3,32,1536]{2,1,0:T(8,128)(2,1)} %in_codes.1, f32[3,12]{1,0:T(4,128)} %in_scales.1, bf16[3,32,768]{2,1,0:T(8,128)(2,1)} %out_codes.1, f32[3,6]{1,0:T(4,128)} %out_scales.1, ...), custom_call_target="tpu_custom_call" | custom-call | tf_op jit(solution)/shard_map/layer/pallas_call | solution.py:559
  39.4 6.0 %finish.1 = bf16[1024,1536]{1,0:T(8,128)(2,1)} custom-call(bf16[1024,1536]{1,0:T(8,128)(2,1)} %bitcast.3, bf16[2048,768]{1,0:T(8,128)(2,1)} %get-tuple-element.7.gated_source, bf16[768,768]{1,0:T(8,128)(2,1)} %get-tuple-element.8.weight_source), custom_call_target="tpu_custom_call" | custom-call | tf_op jit(solution)/shard_map/finish/pallas_call | solution.py:618

commit v5 on v4

--- a/solution.py
+++ b/solution.py
@@ -13,7 +13,7 @@
 ROWS, HALO = 1024, 144
 WIDTH, SHARD = 768, 96
 BLOCK, SPAN = 128, 256
-TILE = 256
+TILE, PART = 512, 256
 DP, CTX = 8, 32
 LONG, SHORT = 128, 4
 VMEM_LIMIT = 63 << 20
@@ -343,11 +343,11 @@
         mean = jnp.mean(wide * wide, axis=-1, keepdims=True)
         return (wide * lax.rsqrt(mean + 1e-5)).astype(BF16)
 
-    def norm_pass(tile, carry):
-        rows = pl.ds(pl.multiple_of(tile * TILE, TILE), TILE)
+    def norm_pass(part, carry):
+        rows = pl.ds(pl.multiple_of(part * PART, PART), PART)
         for strand in range(2):
-            start = (2 * tile + strand) * TILE
-            normed[pl.ds(pl.multiple_of(start, TILE), TILE)] = project(state[strand, rows])
+            start = part // 2 * (2 * TILE) + strand * TILE + part % 2 * PART
+            normed[pl.ds(pl.multiple_of(start, PART), PART)] = project(state[strand, rows])
         return carry
 
     relay(0)
@@ -392,28 +392,16 @@
         copy.wait()
     complete(0)
 
-    def rows_in(tile):
-        return pl.ds(pl.multiple_of(tile * 2 * TILE, TILE), 2 * TILE)
-
-    def value_part(norm, flags):
-        return (dot(norm, weights[0]) * jnp.tile(flags, (1, 6))).astype(BF16)
-
-    def value_pass(tile, carry):
-        start = pl.multiple_of(tile * TILE, TILE)
-        rows = rows_in(tile)
-        values = dot(normed[rows], weights[0])
-        flags = jnp.tile(keep[pl.ds(start + 256, TILE)], (1, 6))
-        masked_forward[pl.ds(pl.multiple_of(start + HALO, 16), TILE)] = (
-            values[:TILE] * flags
-        ).astype(BF16)
-        masked_backward[pl.ds(start, TILE)] = (values[TILE:] * flags).astype(BF16)
-        return carry
-
-    lax.fori_loop(0, 2, value_pass, 0)
+    def value_tile(tile, count):
+        start = tile * TILE
+        values = dot(normed[2 * start : 2 * start + count], weights[0])
+        flags = jnp.tile(keep[start + 256 : start + 256 + TILE], (1, 6))
+        masked_forward[start + HALO : start + HALO + TILE] = (values[:TILE] * flags).astype(BF16)
+        masked_backward[start : start + TILE] = (values[TILE : 2 * TILE] * flags).astype(BF16)
+        return values[2 * TILE :]
+
+    value_tile(0, 2 * TILE)
     share(1)
-    lax.fori_loop(2, ROWS // TILE, value_pass, 0)
-    share(2)
-
     for copy in halos:
         copy.wait_recv()
     live_before = jnp.where(ctx > 0, 1.0, 0.0)
@@ -424,15 +412,17 @@
         keep[ROWS + 256 + block * 128 : ROWS + 384 + block * 128] = keep_rows(
             token_backward[:, columns], live_after
         )
-    masked_forward[0:HALO] = value_part(project(halo_forward[...]), keep[256 - HALO : 256])
-    masked_backward[ROWS : ROWS + HALO] = value_part(
-        project(halo_backward[...]), keep[ROWS + 256 : ROWS + 256 + HALO]
-    )
-    complete(1)
+    normed[2 * ROWS : 2 * ROWS + HALO] = project(halo_forward[...])
+    normed[2 * ROWS + HALO :] = project(halo_backward[...])
+    rims = value_tile(1, 2 * TILE + 2 * HALO)
+    masked_forward[:HALO] = (rims[:HALO] * jnp.tile(keep[256 - HALO : 256], (1, 6))).astype(BF16)
+    masked_backward[ROWS:] = (
+        rims[HALO:] * jnp.tile(keep[ROWS + 256 : ROWS + 256 + HALO], (1, 6))
+    ).astype(BF16)
 
     def filtered(strand, start, target):
         masked = masked_backward if strand else masked_forward
-        origin = start if strand else pl.multiple_of(start + 16, 16)
+        origin = start if strand else start + 16
         window = masked[pl.ds(origin, SPAN)]
         waves = dot(spread[...], window)
         real, imag = waves[:BLOCK], waves[BLOCK:]
@@ -449,7 +439,7 @@
         row = lax.broadcasted_iota(jnp.int32, (8, WIDTH), 0)
         if strand:
             wrong = masked[pl.ds(start, 16)].astype(F32)
-            right = masked[pl.ds(pl.multiple_of(start + SPAN, 16), 16)].astype(F32)
+            right = masked[pl.ds(start + SPAN, 16)].astype(F32)
             gap = right - wrong
             outer, inner = gap[0:1], gap[1:2]
             fix = jnp.where(row == 7, second * outer + last * inner, 0.0)
@@ -457,7 +447,7 @@
             conv[target + BLOCK - 8 : target + BLOCK] += fix
         else:
             right = masked[pl.ds(start, 16)].astype(F32)
-            wrong = masked[pl.ds(pl.multiple_of(start + SPAN, 16), 16)].astype(F32)
+            wrong = masked[pl.ds(start + SPAN, 16)].astype(F32)
             gap = right - wrong
             outer, inner = gap[15:16], gap[14:15]
             fix = jnp.where(row == 0, second * outer + last * inner, 0.0)
@@ -465,27 +455,30 @@
             conv[target : target + 8] += fix
 
     def store(tile):
-        rows = rows_in(tile)
+        rows = pl.ds(tile * 2 * TILE, 2 * TILE)
         return pltpu.make_async_copy(normed.at[rows], gated_out.at[rows], store_sem.at[tile])
 
-    def gate_pass(tile, carry):
-        start = pl.multiple_of(tile * TILE, TILE)
-        rows = rows_in(tile)
+    def conv_tile(tile):
         for strand in range(2):
-            for block in range(TILE // BLOCK):
-                offset = block * BLOCK
-                filtered(strand, pl.multiple_of(start + offset, BLOCK), strand * TILE + offset)
+            for offset in range(0, TILE, BLOCK):
+                filtered(strand, tile * TILE + offset, strand * TILE + offset)
+
+    def gate_tile(tile):
+        rows = slice(tile * 2 * TILE, (tile + 1) * 2 * TILE)
         half_gate = 0.5 * dot(normed[rows], weights[1])
         gated = (half_gate * jnp.tanh(half_gate) + half_gate) * conv[...]
         normed[rows] = gated.astype(BF16)
         store(tile).start()
-        return carry
-
-    lax.fori_loop(0, 3, gate_pass, 0)
+
+    conv_tile(0)
+    share(2)
+    complete(1)
+    gate_tile(0)
+    conv_tile(1)
     complete(2)
     last_store = pltpu.make_async_copy(weights.at[2], last_weights, store_sem.at[ROWS // TILE])
     last_store.start()
-    lax.fori_loop(ROWS // TILE - 1, ROWS // TILE, gate_pass, 0)
+    gate_tile(1)
 
     for copy in halos:
         copy.wait_send()
@@ -514,39 +507,45 @@
     hidden, gated_source, weight_source, out, weight, gated, state, load_sem, ready_sem, store_sem
 ):
     def fetch(unit):
-        rows = pl.ds(pl.multiple_of(unit * TILE, TILE), TILE)
-        own = pl.ds(pl.multiple_of(unit * 2 * TILE, TILE), 2 * TILE)
-        return (
-            pltpu.make_async_copy(gated_source.at[own], gated.at[own], load_sem.at[unit]),
-            pltpu.make_async_copy(hidden.at[rows], state.at[rows], ready_sem.at[unit]),
-            pltpu.make_async_copy(state.at[rows], out.at[rows], store_sem.at[unit]),
-        )
-
-    units = ROWS // TILE
-    first = pltpu.make_async_copy(weight_source, weight, load_sem.at[units])
+        rows = pl.ds(pl.multiple_of(unit * PART, PART), PART)
+        own = pl.multiple_of(unit * 2 * PART, PART)
+        loads = [pltpu.make_async_copy(hidden.at[rows], state.at[rows], ready_sem.at[unit])]
+        for strand in range(2):
+            start = unit // 2 * (2 * TILE) + strand * TILE + unit % 2 * PART
+            loads.append(
+                pltpu.make_async_copy(
+                    gated_source.at[pl.ds(pl.multiple_of(start, PART), PART)],
+                    gated.at[pl.ds(own + strand * PART, PART)],
+                    load_sem.at[unit, strand],
+                )
+            )
+        return *loads, pltpu.make_async_copy(state.at[rows], out.at[rows], store_sem.at[unit])
+
+    units = ROWS // PART
+    first = pltpu.make_async_copy(weight_source, weight, load_sem.at[units, 0])
     first.start()
     for unit in range(units):
-        for copy in fetch(unit)[:2]:
+        for copy in fetch(unit)[:-1]:
             copy.start()
     first.wait()
 
     def out_pass(unit, carry):
-        rows = pl.ds(pl.multiple_of(unit * TILE, TILE), TILE)
-        own = pl.ds(pl.multiple_of(unit * 2 * TILE, TILE), 2 * TILE)
+        rows = pl.ds(pl.multiple_of(unit * PART, PART), PART)
+        own = pl.ds(pl.multiple_of(unit * 2 * PART, PART), 2 * PART)
         *loads, store = fetch(unit)
         for copy in loads:
             copy.wait()
         branch = jnp.dot(gated[own], weight[...], preferred_element_type=F32)
         for strand in range(2):
             columns = slice(strand * WIDTH, strand * WIDTH + WIDTH)
-            added = branch[strand * TILE : strand * TILE + TILE]
+            added = branch[strand * PART : strand * PART + PART]
             state[rows, columns] = (state[rows, columns].astype(F32) + added).astype(BF16)
         store.start()
         return carry
 
     lax.fori_loop(0, units, out_pass, 0)
     for unit in range(units):
-        fetch(unit)[2].wait()
+        fetch(unit)[-1].wait()
 
 
 def shards(
@@ -579,7 +578,7 @@
             pltpu.VMEM((LONG, WIDTH), BF16),
             *(pltpu.VMEM(table.shape, BF16) for table in tables),
             pltpu.VMEM((2, ROWS, WIDTH), BF16),
-            pltpu.VMEM((2 * ROWS, WIDTH), BF16),
+            pltpu.VMEM((2 * ROWS + 2 * HALO, WIDTH), BF16),
             pltpu.VMEM((ROWS + HALO, WIDTH), BF16),
             pltpu.VMEM((ROWS + HALO, WIDTH), BF16),
             pltpu.VMEM((ROWS + 512, 128), F32),
@@ -624,7 +623,7 @@
             pltpu.VMEM((WIDTH, WIDTH), BF16),
             pltpu.VMEM((2 * ROWS, WIDTH), BF16),
             pltpu.VMEM((ROWS, 2 * WIDTH), BF16),
-            dma((8,)),
+            dma((ROWS // PART + 1, 2)),
             dma((8,)),
             dma((8,)),
         ],

time: 45.4 us -> 46.4 us (1.022)
  Pallas kernels: 45.4 us -> 46.3 us
    pallas_call x1, Pallas kernels: 39.4 us -> 40.1 us  [shards(): pl.pallas_call(layer_kernel, out_shape=(jax.ShapeDtypeStruct((2 * ROWS, W...]
where the time goes in v5:
time: 46.4 us; the launch traced here: 46.3 us
  Pallas kernels  46.3 us (100%)
    pallas_call x1, Pallas kernels, shards(): pl.pallas_call(layer_kernel, out_shape=(jax.ShapeDtypeStruct((2 * ROWS, W...  40.1 us
    pallas_call x1, Pallas kernels, shards(): pl.pallas_call(finish_kernel, out_shape=jax.ShapeDtypeStruct((ROWS, 2 * W...  6.21 us

profile of v5, /device:TPU:1, one launch (start us, length us, event | category | flops | bytes accessed | tf_op | source)
XLA Modules:
  0.0 46.3 jit_solution(5260891864796522129)
XLA Ops:
  0.0 40.1 %layer.1 = (bf16[2048,768]{1,0:T(8,128)(2,1)}, bf16[768,768]{1,0:T(8,128)(2,1)}) custom-call(bf16[1024,1536]{1,0:T(8,128)(2,1)} %bitcast.2, s32[1,1024]{1,0:T(1,128)} %tokens.1, bf16[3,32,1536]{2,1,0:T(8,128)(2,1)} %in_codes.1, f32[3,12]{1,0:T(4,128)} %in_scales.1, bf16[3,32,768]{2,1,0:T(8,128)(2,1)} %out_codes.1, f32[3,6]{1,0:T(4,128)} %out_scales.1, ...), custom_call_target="tpu_custom_call" | custom-call | tf_op jit(solution)/shard_map/layer/pallas_call | solution.py:558
  40.1 6.2 %finish.1 = bf16[1024,1536]{1,0:T(8,128)(2,1)} custom-call(bf16[1024,1536]{1,0:T(8,128)(2,1)} %bitcast.3, bf16[2048,768]{1,0:T(8,128)(2,1)} %get-tuple-element.7.gated_source, bf16[768,768]{1,0:T(8,128)(2,1)} %get-tuple-element.8.weight_source), custom_call_target="tpu_custom_call" | custom-call | tf_op jit(solution)/shard_map/finish/pallas_call | solution.py:617

commit v6 on v5

--- a/solution.py
+++ b/solution.py
@@ -220,10 +220,9 @@
             cross_recv.at[part, row],
         )
 
-    def to_mate(part, row, side, index):
-        return remote(
-            piece(part, row, side), mate, mate_send.at[part, index], mate_recv.at[part, row]
-        )
+    def to_mate(part, row, index):
+        ref = weights.at[part, pl.ds(pl.multiple_of(base_of(row, core), 32), SHARD)]
+        return remote(ref, mate, mate_send.at[part, index], mate_recv.at[part, row])
 
     def z_copies(part):
         sign = 1 - 2 * (z_low // 3)
@@ -265,27 +264,25 @@
             for copy in ring_copies(part):
                 copy.start()
             aside(part, y, 0).start()
-            to_mate(part, y, half, 0).start()
 
     def collect(part):
         for index, row in enumerate((below, above, across)):
             along(part, row, up, 0).wait_recv()
             aside(part, row, index + 1).start()
-            to_mate(part, row, half, 2 * index + 2).start()
 
     def share(part):
         def pass_on(row, index):
             remote(
                 piece(part, row, 1 - half), beside, x_send.at[part, 0], cross_recv.at[part, row]
             ).wait_recv()
-            to_mate(part, row, 1 - half, index).start()
+            to_mate(part, row, index).start()
 
         @pl.when(fetches == 1)
         def _():
-            pass_on(y, 1)
+            pass_on(y, 0)
 
         for index, row in enumerate((below, above, across)):
-            pass_on(row, 2 * index + 3)
+            pass_on(row, index + 1)
 
     def complete(part):
         def finish(row):
@@ -314,19 +311,22 @@
         copy.start()
         halos.append(copy)
 
-    z_owner(0, start)
-    ring_owner(0, start)
+    def open_part(part):
+        z_owner(part, start)
+        ring_owner(part, start)
+
+    open_part(0)
+    for copy in last_loads:
+        copy.wait()
+    dequantise(1)
+    open_part(1)
+    dequantise(2)
+    open_part(2)
     letter_load.wait()
     halo(letters.at[:, pl.ds(ROWS - 256, 256)], token_forward, after)
     halo(letters.at[:, pl.ds(0, 256)], token_backward, before)
     halo(hidden.at[pl.ds(ROWS - HALO, HALO), pl.ds(0, WIDTH)], halo_forward, after)
     halo(hidden.at[pl.ds(0, HALO), pl.ds(WIDTH, WIDTH)], halo_backward, before)
-    for copy in last_loads:
-        copy.wait()
-    dequantise(1)
-    z_owner(0, sent)
-    z_owner(1, start)
-    dequantise(2)
 
     def keep_rows(values, live):
         flags = jnp.where(values != 4, live, 0.0)
@@ -350,23 +350,16 @@
             normed[pl.ds(pl.multiple_of(start, PART), PART)] = project(state[strand, rows])
         return carry
 
-    relay(0)
-    z_owner(1, sent)
-    z_owner(2, start)
     for copy in state_loads:
         copy.wait()
     lax.fori_loop(0, 1, norm_pass, 0)
+    relay(0)
+    lax.fori_loop(1, 3, norm_pass, 0)
     relay(1)
-    ring_owner(1, start)
-    lax.fori_loop(1, 2, norm_pass, 0)
+    lax.fori_loop(3, 4, norm_pass, 0)
     relay(2)
     collect(0)
-    ring_owner(2, start)
-    lax.fori_loop(2, 3, norm_pass, 0)
     collect(1)
-    lax.fori_loop(3, 4, norm_pass, 0)
-    collect(2)
-    share(0)
 
     for copy in filter_loads:
         copy.wait()
@@ -390,6 +383,8 @@
 
     for copy in table_loads:
         copy.wait()
+    share(0)
+    collect(2)
     complete(0)
 
     def value_tile(tile, count):
@@ -402,6 +397,7 @@
 
     value_tile(0, 2 * TILE)
     share(1)
+    share(2)
     for copy in halos:
         copy.wait_recv()
     live_before = jnp.where(ctx > 0, 1.0, 0.0)
@@ -422,7 +418,7 @@
 
     def filtered(strand, start, target):
         masked = masked_backward if strand else masked_forward
-        origin = start if strand else start + 16
+        origin = start if strand else pl.multiple_of(start + 16, 16)
         window = masked[pl.ds(origin, SPAN)]
         waves = dot(spread[...], window)
         real, imag = waves[:BLOCK], waves[BLOCK:]
@@ -439,7 +435,7 @@
         row = lax.broadcasted_iota(jnp.int32, (8, WIDTH), 0)
         if strand:
             wrong = masked[pl.ds(start, 16)].astype(F32)
-            right = masked[pl.ds(start + SPAN, 16)].astype(F32)
+            right = masked[pl.ds(pl.multiple_of(start + SPAN, 16), 16)].astype(F32)
             gap = right - wrong
             outer, inner = gap[0:1], gap[1:2]
             fix = jnp.where(row == 7, second * outer + last * inner, 0.0)
@@ -447,43 +443,40 @@
             conv[target + BLOCK - 8 : target + BLOCK] += fix
         else:
             right = masked[pl.ds(start, 16)].astype(F32)
-            wrong = masked[pl.ds(start + SPAN, 16)].astype(F32)
+            wrong = masked[pl.ds(pl.multiple_of(start + SPAN, 16), 16)].astype(F32)
             gap = right - wrong
             outer, inner = gap[15:16], gap[14:15]
             fix = jnp.where(row == 0, second * outer + last * inner, 0.0)
             fix = fix + jnp.where(row == 1, last * outer, 0.0)
             conv[target : target + 8] += fix
 
+    complete(1)
+
     def store(tile):
-        rows = pl.ds(tile * 2 * TILE, 2 * TILE)
+        rows = pl.ds(pl.multiple_of(tile * 2 * TILE, TILE), 2 * TILE)
         return pltpu.make_async_copy(normed.at[rows], gated_out.at[rows], store_sem.at[tile])
 
-    def conv_tile(tile):
+    def gate_pass(tile, carry):
+        start = pl.multiple_of(tile * TILE, TILE)
+        rows = pl.ds(pl.multiple_of(tile * 2 * TILE, TILE), 2 * TILE)
         for strand in range(2):
             for offset in range(0, TILE, BLOCK):
-                filtered(strand, tile * TILE + offset, strand * TILE + offset)
-
-    def gate_tile(tile):
-        rows = slice(tile * 2 * TILE, (tile + 1) * 2 * TILE)
+                filtered(strand, pl.multiple_of(start + offset, BLOCK), strand * TILE + offset)
         half_gate = 0.5 * dot(normed[rows], weights[1])
         gated = (half_gate * jnp.tanh(half_gate) + half_gate) * conv[...]
         normed[rows] = gated.astype(BF16)
         store(tile).start()
-
-    conv_tile(0)
-    share(2)
-    complete(1)
-    gate_tile(0)
-    conv_tile(1)
+        return carry
+
+    lax.fori_loop(0, ROWS // TILE, gate_pass, 0)
     complete(2)
     last_store = pltpu.make_async_copy(weights.at[2], last_weights, store_sem.at[ROWS // TILE])
     last_store.start()
-    gate_tile(1)
 
     for copy in halos:
         copy.wait_send()
-    z_owner(2, sent)
     for part in range(3):
+        z_owner(part, sent)
         ring_owner(part, sent)
 
         @pl.when(fetches == 1)
@@ -491,13 +484,11 @@
             for copy in ring_copies(part):
                 copy.wait_send()
             aside(part, y, 0).wait_send()
-            for side in range(2):
-                to_mate(part, y, side, side).wait_send()
+            to_mate(part, y, 0).wait_send()
 
         for index, row in enumerate((below, above, across)):
             aside(part, row, index + 1).wait_send()
-            for side in range(2):
-                to_mate(part, row, side, 2 * index + 2 + side).wait_send()
+            to_mate(part, row, index + 1).wait_send()
     for tile in range(ROWS // TILE):
         store(tile).wait()
     last_store.wait()
@@ -596,7 +587,7 @@
             dma((3, 2)),
             dma((3, 3)),
             dma((3, 4)),
-            dma((3, 8)),
+            dma((3, 4)),
             dma((4,)),
         ],
         compiler_params=pltpu.CompilerParams(

time: 46.4 us -> 45 us (0.970)
  Pallas kernels: 46.3 us -> 45 us
    pallas_call x1, Pallas kernels: 40.1 us -> 38.7 us  [shards(): pl.pallas_call(layer_kernel, out_shape=(jax.ShapeDtypeStruct((2 * ROWS, W...]
where the time goes in v6:
time: 45 us
  Pallas kernels  45 us (100%)
    pallas_call x1, Pallas kernels, shards(): pl.pallas_call(layer_kernel, out_shape=(jax.ShapeDtypeStruct((2 * ROWS, W...  38.7 us
    pallas_call x1, Pallas kernels, shards(): pl.pallas_call(finish_kernel, out_shape=jax.ShapeDtypeStruct((ROWS, 2 * W...  6.21 us

profile of v6, /device:TPU:1, one launch (start us, length us, event | category | flops | bytes accessed | tf_op | source)
XLA Modules:
  0.0 45.0 jit_solution(6904486714364100953)
XLA Ops:
  0.0 38.7 %layer.1 = (bf16[2048,768]{1,0:T(8,128)(2,1)}, bf16[768,768]{1,0:T(8,128)(2,1)}) custom-call(bf16[1024,1536]{1,0:T(8,128)(2,1)} %bitcast.2, s32[1,1024]{1,0:T(1,128)} %tokens.1, bf16[3,32,1536]{2,1,0:T(8,128)(2,1)} %in_codes.1, f32[3,12]{1,0:T(4,128)} %in_scales.1, bf16[3,32,768]{2,1,0:T(8,128)(2,1)} %out_codes.1, f32[3,6]{1,0:T(4,128)} %out_scales.1, ...), custom_call_target="tpu_custom_call" | custom-call | tf_op jit(solution)/shard_map/layer/pallas_call | solution.py:549
  38.7 6.2 %finish.1 = bf16[1024,1536]{1,0:T(8,128)(2,1)} custom-call(bf16[1024,1536]{1,0:T(8,128)(2,1)} %bitcast.3, bf16[2048,768]{1,0:T(8,128)(2,1)} %get-tuple-element.7.gated_source, bf16[768,768]{1,0:T(8,128)(2,1)} %get-tuple-element.8.weight_source), custom_call_target="tpu_custom_call" | custom-call | tf_op jit(solution)/shard_map/finish/pallas_call | solution.py:608

commit v7 on v6

--- a/solution.py
+++ b/solution.py
@@ -233,7 +233,7 @@
                 z_send.at[part, index],
                 piece_recv.at[part, y],
             )
-            for index, distance in enumerate((16, 24))
+            for index, distance in enumerate((24, 16))
         ]
 
     def ring_copies(part):
@@ -357,8 +357,8 @@
     lax.fori_loop(1, 3, norm_pass, 0)
     relay(1)
     lax.fori_loop(3, 4, norm_pass, 0)
+    collect(0)
     relay(2)
-    collect(0)
     collect(1)
 
     for copy in filter_loads:
@@ -384,7 +384,6 @@
     for copy in table_loads:
         copy.wait()
     share(0)
-    collect(2)
     complete(0)
 
     def value_tile(tile, count):
@@ -396,8 +395,8 @@
         return values[2 * TILE :]
 
     value_tile(0, 2 * TILE)
+    collect(2)
     share(1)
-    share(2)
     for copy in halos:
         copy.wait_recv()
     live_before = jnp.where(ctx > 0, 1.0, 0.0)
@@ -468,7 +467,9 @@
         store(tile).start()
         return carry
 
-    lax.fori_loop(0, ROWS // TILE, gate_pass, 0)
+    lax.fori_loop(0, 1, gate_pass, 0)
+    share(2)
+    lax.fori_loop(1, ROWS // TILE, gate_pass, 0)
     complete(2)
     last_store = pltpu.make_async_copy(weights.at[2], last_weights, store_sem.at[ROWS // TILE])
     last_store.start()

time: 45 us -> 45.1 us (level)
  no operation moved by 1% of the time
where the time goes in v7:
time: 45.1 us
  Pallas kernels  45.1 us (100%)
    pallas_call x1, Pallas kernels, shards(): pl.pallas_call(layer_kernel, out_shape=(jax.ShapeDtypeStruct((2 * ROWS, W...  38.8 us
    pallas_call x1, Pallas kernels, shards(): pl.pallas_call(finish_kernel, out_shape=jax.ShapeDtypeStruct((ROWS, 2 * W...  6.21 us

profile of v7, /device:TPU:1, one launch (start us, length us, event | category | flops | bytes accessed | tf_op | source)
XLA Modules:
  0.0 45.1 jit_solution(6250117511353995463)
XLA Ops:
  0.0 38.8 %layer.1 = (bf16[2048,768]{1,0:T(8,128)(2,1)}, bf16[768,768]{1,0:T(8,128)(2,1)}) custom-call(bf16[1024,1536]{1,0:T(8,128)(2,1)} %bitcast.2, s32[1,1024]{1,0:T(1,128)} %tokens.1, bf16[3,32,1536]{2,1,0:T(8,128)(2,1)} %in_codes.1, f32[3,12]{1,0:T(4,128)} %in_scales.1, bf16[3,32,768]{2,1,0:T(8,128)(2,1)} %out_codes.1, f32[3,6]{1,0:T(4,128)} %out_scales.1, ...), custom_call_target="tpu_custom_call" | custom-call | tf_op jit(solution)/shard_map/layer/pallas_call | solution.py:550
  38.9 6.2 %finish.1 = bf16[1024,1536]{1,0:T(8,128)(2,1)} custom-call(bf16[1024,1536]{1,0:T(8,128)(2,1)} %bitcast.3, bf16[2048,768]{1,0:T(8,128)(2,1)} %get-tuple-element.7.gated_source, bf16[768,768]{1,0:T(8,128)(2,1)} %get-tuple-element.8.weight_source), custom_call_target="tpu_custom_call" | custom-call | tf_op jit(solution)/shard_map/finish/pallas_call | solution.py:609

commit v8 on v7

--- a/solution.py
+++ b/solution.py
@@ -449,30 +449,34 @@
             fix = fix + jnp.where(row == 1, last * outer, 0.0)
             conv[target : target + 8] += fix
 
-    complete(1)
-
     def store(tile):
         rows = pl.ds(pl.multiple_of(tile * 2 * TILE, TILE), 2 * TILE)
         return pltpu.make_async_copy(normed.at[rows], gated_out.at[rows], store_sem.at[tile])
 
-    def gate_pass(tile, carry):
+    def conv_pass(tile, carry):
         start = pl.multiple_of(tile * TILE, TILE)
-        rows = pl.ds(pl.multiple_of(tile * 2 * TILE, TILE), 2 * TILE)
         for strand in range(2):
             for offset in range(0, TILE, BLOCK):
                 filtered(strand, pl.multiple_of(start + offset, BLOCK), strand * TILE + offset)
+        return carry
+
+    def gate_pass(tile, carry):
+        rows = pl.ds(pl.multiple_of(tile * 2 * TILE, TILE), 2 * TILE)
         half_gate = 0.5 * dot(normed[rows], weights[1])
         gated = (half_gate * jnp.tanh(half_gate) + half_gate) * conv[...]
         normed[rows] = gated.astype(BF16)
         store(tile).start()
         return carry
 
+    lax.fori_loop(0, 1, conv_pass, 0)
+    complete(1)
     lax.fori_loop(0, 1, gate_pass, 0)
     share(2)
-    lax.fori_loop(1, ROWS // TILE, gate_pass, 0)
+    lax.fori_loop(1, ROWS // TILE, conv_pass, 0)
     complete(2)
     last_store = pltpu.make_async_copy(weights.at[2], last_weights, store_sem.at[ROWS // TILE])
     last_store.start()
+    lax.fori_loop(1, ROWS // TILE, gate_pass, 0)
 
     for copy in halos:
         copy.wait_send()

time: 45.1 us -> 44.8 us (level)
  no operation moved by 1% of the time
where the time goes in v8:
time: 44.8 us; the launch traced here: 44.7 us
  Pallas kernels  44.7 us (100%)
    pallas_call x1, Pallas kernels, shards(): pl.pallas_call(layer_kernel, out_shape=(jax.ShapeDtypeStruct((2 * ROWS, W...  38.5 us
    pallas_call x1, Pallas kernels, shards(): pl.pallas_call(finish_kernel, out_shape=jax.ShapeDtypeStruct((ROWS, 2 * W...  6.21 us

profile of v8, /device:TPU:1, one launch (start us, length us, event | category | flops | bytes accessed | tf_op | source)
XLA Modules:
  0.0 44.7 jit_solution(557826212831206875)
XLA Ops:
  0.0 38.5 %layer.1 = (bf16[2048,768]{1,0:T(8,128)(2,1)}, bf16[768,768]{1,0:T(8,128)(2,1)}) custom-call(bf16[1024,1536]{1,0:T(8,128)(2,1)} %bitcast.2, s32[1,1024]{1,0:T(1,128)} %tokens.1, bf16[3,32,1536]{2,1,0:T(8,128)(2,1)} %in_codes.1, f32[3,12]{1,0:T(4,128)} %in_scales.1, bf16[3,32,768]{2,1,0:T(8,128)(2,1)} %out_codes.1, f32[3,6]{1,0:T(4,128)} %out_scales.1, ...), custom_call_target="tpu_custom_call" | custom-call | tf_op jit(solution)/shard_map/layer/pallas_call | solution.py:554
  38.5 6.2 %finish.1 = bf16[1024,1536]{1,0:T(8,128)(2,1)} custom-call(bf16[1024,1536]{1,0:T(8,128)(2,1)} %bitcast.3, bf16[2048,768]{1,0:T(8,128)(2,1)} %get-tuple-element.7.gated_source, bf16[768,768]{1,0:T(8,128)(2,1)} %get-tuple-element.8.weight_source), custom_call_target="tpu_custom_call" | custom-call | tf_op jit(solution)/shard_map/finish/pallas_call | solution.py:613
